TPU v7x, 128 devices: a whole 4x4x4 slice. The times are simulated.
128 devices in a mesh: dp: 32 (over z, y_lo, x), tensor: 4 (over y_hi, core).
Axes of the slice: x: 4, y: 4 (y_hi: 2, y_lo: 2; y = y_hi * 2 + y_lo), z: 4, core: 2. Of those that a mesh axis runs over, the one named last changes fastest.
Arguments:
- layer_input: bfloat16 [49152, 768], P('dp'), may hold values from -6 to 6
- flags: int32 [49152], P('dp'), may hold values from 0 to 1, as said below
- loss_mask: int32 [49152], P('dp'), may hold values 0 or 1
- cotangent: bfloat16 [49152, 768], P('dp'), may hold values from -6 to 6
- gain_one: float32 [768], replicated, may hold values from 0.5 to 1.5
- shift_one: float32 [768], replicated, may hold values from -1.8 to 1.8
- w_qkv: bfloat16 [3, 768, 768], P(None, None, 'tensor'), may hold values from -0.21875 to 0.21875
- b_qv: float32 [2, 768], P(None, 'tensor'), may hold values from -1.8 to 1.8
- w_out: bfloat16 [768, 768], P('tensor'), may hold values from -0.875 to 0.875
- b_out: float32 [768], replicated, may hold values from -1.8 to 1.8
- gain_two: float32 [768], replicated, may hold values from 0.5 to 1.5
- shift_two: float32 [768], replicated, may hold values from -1.8 to 1.8
- w_up: bfloat16 [768, 3072], P(None, 'tensor'), may hold values from -0.21875 to 0.21875
- b_up: float32 [3072], P('tensor'), may hold values from -3 to 3
- w_down: bfloat16 [3072, 768], P('tensor'), may hold values from -0.109375 to 0.109375
- b_down: float32 [768], replicated, may hold values from -1.8 to 1.8
Outputs:
- output: bfloat16 [49152, 768], P('dp')
- grad_input: bfloat16 [49152, 768], P('dp')
- grad_gain_one: float32 [768], replicated
- grad_shift_one: float32 [768], replicated
- grad_w_qkv: float32 [3, 768, 768], P(None, None, 'tensor')
- grad_b_qv: float32 [2, 768], P(None, 'tensor')
- grad_w_out: float32 [768, 768], P('tensor')
- grad_b_out: float32 [768], replicated
- grad_gain_two: float32 [768], replicated
- grad_shift_two: float32 [768], replicated
- grad_w_up: float32 [768, 3072], P(None, 'tensor')
- grad_b_up: float32 [3072], P('tensor')
- grad_w_down: float32 [3072, 768], P('tensor')
- grad_b_down: float32 [768], replicated
Inputs may be any that keep to these rules, and one draw needn't show every extreme that they name: Within each sequence of 512 consecutive rows the flags are 1 on a leading run of 1 to 511 rows and 0 after it.
All inputs are finite; a program needn't handle non-finite values. No bound on the sum of `loss_mask` on one device may be relied on, other than what follows from the above.
Results may differ from a plain program's by a relative error of at most 0.01.
Values may be sent and summed in bfloat16 or wider, within the bound.
A program may use at most 192 MiB of HBM per device.

v0:
```python
import jax
import jax.numpy as jnp
from jax import lax
from jax.sharding import PartitionSpec as P

HDIM = 64
LEN = 512


epsilon = 1e-05


def laid_out(pieces, dim):
    lengths = list(pieces.shape[1:])
    lengths[dim] *= pieces.shape[0]
    return jnp.moveaxis(pieces, 0, dim).reshape(lengths)


def sent_to_all(array, axis):
    copies = jnp.broadcast_to(array, (lax.axis_size(axis), *array.shape))
    return lax.all_to_all(copies, axis, split_axis=0, concat_axis=0, tiled=True)


def gather_directly(array, axis, dim):
    return laid_out(sent_to_all(array, axis), dim)


def in_blocks(array, dim, count):
    before, after = (array.shape[:dim], array.shape[dim + 1 :])
    return jnp.moveaxis(array.reshape(*before, count, -1, *after), dim, 0)


def summed_on_arrival(array, axis, dim):
    count = lax.axis_size(axis)
    pieces = lax.all_to_all(in_blocks(array, dim, count), axis, 0, 0, tiled=True)
    return jnp.sum(pieces.astype(jnp.float32), axis=0)


def sum_at_owner(array, axis, dim):
    pieces = in_blocks(array, dim, lax.axis_size(axis))
    arrived = lax.all_to_all(pieces, axis, split_axis=0, concat_axis=0, tiled=True)
    return arrived.sum(axis=0)


def layer_norm(source, scaling, offset):
    average = jnp.mean(source, axis=-1, keepdims=True)
    centred = source - average
    spread = jnp.mean(centred * centred, axis=-1, keepdims=True)
    return centred * lax.rsqrt(spread + epsilon) * scaling + offset


def norm_back(source, scaling, offset, incoming):
    unused, pullback = jax.vjp(layer_norm, source, scaling, offset)
    return pullback(incoming)


def attend(queries, keys_all, values_all, score_scale):
    scores = (
        jnp.einsum("slhe,smhe->shlm", queries, keys_all, preferred_element_type=jnp.float32)
        * score_scale
    )
    row_top = jnp.max(scores, axis=-1, keepdims=True)
    exponent = jnp.exp(scores - row_top)
    expo_total = jnp.sum(exponent, axis=-1, keepdims=True)
    log_total = row_top + jnp.log(expo_total)
    prob_low = (exponent / expo_total).astype(jnp.bfloat16)
    mixed_out = jnp.einsum(
        "shlm,smhe->slhe", prob_low, values_all, preferred_element_type=jnp.float32
    )
    return (mixed_out, log_total)


def attend_back(queries, keys_all, values_all, log_total, grad_mixed, score_scale):
    scores = (
        jnp.einsum("slhe,smhe->shlm", queries, keys_all, preferred_element_type=jnp.float32)
        * score_scale
    )
    prob_full = jnp.exp(scores - log_total)
    prob_low = prob_full.astype(jnp.bfloat16)
    grad_values = jnp.einsum(
        "shlm,slhe->smhe", prob_low, grad_mixed, preferred_element_type=jnp.float32
    )
    grad_probs = jnp.einsum(
        "slhe,smhe->shlm", grad_mixed, values_all, preferred_element_type=jnp.float32
    )
    row_dot = jnp.sum(grad_probs * prob_full, axis=-1, keepdims=True)
    grad_scores = (prob_full * (grad_probs - row_dot)).astype(jnp.bfloat16)
    grad_queries = (
        jnp.einsum("shlm,smhe->slhe", grad_scores, keys_all, preferred_element_type=jnp.float32)
        * score_scale
    )
    grad_keys = (
        jnp.einsum("shlm,slhe->smhe", grad_scores, queries, preferred_element_type=jnp.float32)
        * score_scale
    )
    return (grad_queries, grad_keys, grad_values)


def shards(
    layer_input,
    flags,
    loss_mask,
    cotangent,
    gain_one,
    shift_one,
    w_qkv,
    b_qv,
    w_out,
    b_out,
    gain_two,
    shift_two,
    w_up,
    b_up,
    w_down,
    b_down,
):
    inputs = layer_input.astype(jnp.float32)
    row_count = inputs.shape[0]
    local_heads = w_qkv.shape[2] // HDIM
    seq_count = row_count // LEN
    score_scale = HDIM ** (-0.5)
    row_share = row_count // lax.axis_size("tensor")
    row_start = lax.axis_index("tensor") * row_share
    normed_one = layer_norm(inputs, gain_one, shift_one).astype(jnp.bfloat16)
    projected = jnp.einsum("rd,cde->cre", normed_one, w_qkv, preferred_element_type=jnp.float32)
    bias_rows = jnp.stack([b_qv[0], jnp.zeros_like(b_qv[0]), b_qv[1]])
    biased = (projected + bias_rows[:, None, :]).astype(jnp.bfloat16)
    shaped = biased.reshape(3, seq_count, LEN, local_heads, HDIM)
    attention, log_total = attend(shaped[0], shaped[1], shaped[2], score_scale)
    attended = attention.reshape(row_count, local_heads * HDIM).astype(jnp.bfloat16)
    branch = jnp.dot(attended, w_out, preferred_element_type=jnp.float32)
    input_rows = lax.dynamic_slice_in_dim(inputs, row_start, row_share, 0)
    middle_rows = (
        input_rows + lax.psum_scatter(branch, "tensor", scatter_dimension=0, tiled=True) + b_out
    )
    normed_local = layer_norm(middle_rows, gain_two, shift_two).astype(jnp.bfloat16)
    normed_two = gather_directly(normed_local, "tensor", 0)
    hidden = jnp.dot(normed_two, w_up, preferred_element_type=jnp.float32) + b_up
    activated = jax.nn.gelu(hidden).astype(jnp.bfloat16)
    down_part = jnp.dot(activated, w_down, preferred_element_type=jnp.float32)
    result_rows = (
        middle_rows + summed_on_arrival(down_part.astype(jnp.bfloat16), "tensor", 0) + b_down
    )
    output = gather_directly(result_rows.astype(jnp.bfloat16), "tensor", 0)
    weighting = jnp.maximum(flags, loss_mask).astype(jnp.float32)
    upstream = cotangent.astype(jnp.float32) * weighting[:, None]
    upstream_low = upstream.astype(jnp.bfloat16)
    grad_w_down = jnp.einsum(
        "rf,rd->fd", activated, upstream_low, preferred_element_type=jnp.float32
    )
    grad_act = jnp.einsum("rd,fd->rf", upstream_low, w_down, preferred_element_type=jnp.float32)
    unused, gelu_pull = jax.vjp(jax.nn.gelu, hidden)
    grad_hidden = gelu_pull(grad_act)[0]
    grad_b_up = jnp.sum(grad_hidden, axis=0)
    grad_hidden_low = grad_hidden.astype(jnp.bfloat16)
    grad_w_up = jnp.einsum(
        "rd,rf->df", normed_two, grad_hidden_low, preferred_element_type=jnp.float32
    )
    normed_back = jnp.einsum("rf,df->rd", grad_hidden_low, w_up, preferred_element_type=jnp.float32)
    normed_part = lax.psum_scatter(normed_back, "tensor", scatter_dimension=0, tiled=True)
    grad_mid_norm, grad_gain_two, grad_shift_two = norm_back(
        middle_rows, gain_two, shift_two, normed_part
    )
    upstream_rows = lax.dynamic_slice_in_dim(upstream, row_start, row_share, 0)
    grad_middle_rows = upstream_rows + grad_mid_norm
    grad_b_down = jnp.sum(upstream_rows, axis=0)
    grad_b_out = jnp.sum(grad_middle_rows, axis=0)
    middle_low = lax.all_gather(grad_middle_rows.astype(jnp.bfloat16), "tensor", axis=0, tiled=True)
    grad_w_out = jnp.einsum("re,rd->ed", attended, middle_low, preferred_element_type=jnp.float32)
    grad_attended = jnp.einsum(
        "rd,ed->re", middle_low, w_out, preferred_element_type=jnp.float32
    ).astype(jnp.bfloat16)
    grad_mixed = grad_attended.reshape(seq_count, LEN, local_heads, HDIM)
    grad_queries, grad_keys, grad_values = attend_back(
        shaped[0], shaped[1], shaped[2], log_total, grad_mixed, score_scale
    )
    stacked = (
        jnp.stack([grad_queries, grad_keys, grad_values])
        .reshape(3, row_count, local_heads * HDIM)
        .astype(jnp.bfloat16)
    )
    grad_b_qv = jnp.stack(
        [
            jnp.sum(stacked[0].astype(jnp.float32), axis=0),
            jnp.sum(stacked[2].astype(jnp.float32), axis=0),
        ]
    )
    grad_w_qkv = jnp.einsum("rd,cre->cde", normed_one, stacked, preferred_element_type=jnp.float32)
    normed_back_one = jnp.einsum("cre,cde->rd", stacked, w_qkv, preferred_element_type=jnp.float32)
    normed_part_one = sum_at_owner(normed_back_one, "tensor", 0)
    grad_in_norm, grad_gain_one, grad_shift_one = norm_back(
        input_rows, gain_one, shift_one, normed_part_one
    )
    grad_input = lax.all_gather(
        (grad_middle_rows + grad_in_norm).astype(jnp.bfloat16), "tensor", axis=0, tiled=True
    )
    summed = lax.psum(
        (
            grad_w_qkv,
            grad_b_qv,
            grad_w_out,
            grad_w_up,
            grad_b_up,
            grad_w_down,
            grad_gain_one,
            grad_shift_one,
            grad_b_out,
            grad_gain_two,
            grad_shift_two,
            grad_b_down,
        ),
        "dp",
    )
    small_sums = lax.psum(
        (summed[6], summed[7], summed[8], summed[9], summed[10], summed[11]), "tensor"
    )
    return (
        output,
        grad_input,
        small_sums[0],
        small_sums[1],
        summed[0],
        summed[1],
        summed[2],
        small_sums[2],
        small_sums[3],
        small_sums[4],
        summed[3],
        summed[4],
        summed[5],
        small_sums[5],
    )


def solution(mesh):
    in_specs = (
        P("dp", None),
        P("dp"),
        P("dp"),
        P("dp", None),
        P(),
        P(),
        P(None, None, "tensor"),
        P(None, "tensor"),
        P("tensor", None),
        P(),
        P(),
        P(),
        P(None, "tensor"),
        P("tensor"),
        P("tensor", None),
        P(),
    )
    out_specs = (
        P("dp", None),
        P("dp", None),
        P(),
        P(),
        P(None, None, "tensor"),
        P(None, "tensor"),
        P("tensor", None),
        P(),
        P(),
        P(),
        P(None, "tensor"),
        P("tensor"),
        P("tensor", None),
        P(),
    )
    return jax.shard_map(shards, mesh=mesh, in_specs=in_specs, out_specs=out_specs, check_vma=False)
```

profile of v0, /device:TPU:0, one launch (start us, length us, event | category | flops | bytes accessed | tf_op | source)
XLA Modules:
  0.0 752.6 jit_solution(246012887433635642)
XLA Ops:
  20.9 2.8 multiply_reduce_fusion.1
  31.1 3.1 fusion.67
  34.2 2.5 convert_element_type.75
  38.2 53.4 %reduce-scatter.3.cloned.1.call-done = f32[384,768]{1,0:T(8,128)} async-done(((f32[1536,768]{1,0:T(8,128)}), f32[384,768]{1,0:T(8,128)}) %reduce-scatter.3.cloned.1.call-update) | async-done | bytes 1179664 | tf_op jit(solution)/shard_map/reduce_scatter | solution.py:134
  95.6 4.6 all-to-all-start
  100.5 29.8 %all-to-all-done = bf16[4,384,768]{2,1,0:T(8,128)(2,1)} async-done(((bf16[4,384,768]{2,1,0:T(8,128)(2,1)}), bf16[4,384,768]{2,1,0:T(8,128)(2,1)}, u32[]{:S(2)}, u32[]{:S(2)}) %all-to-all-start) | async-done | bytes 2359328 | tf_op jit(solution)/shard_map/all_to_all | solution.py:21
  130.4 4.1 fusion.68
  134.6 5.7 fusion.66
  141.6 4.3 fusion.35
  145.9 6.8 convolution_convert_fusion
  152.7 4.7 all-to-all-start.1
  157.5 4.4 convert_multiply_fusion
  162.0 40.4 %all-to-all-done.1 = bf16[4,384,768]{2,1,0:T(8,128)(2,1)} async-done(((bf16[4,384,768]{2,1,0:T(8,128)(2,1)}), bf16[4,384,768]{2,1,0:T(8,128)(2,1)}, u32[]{:S(2)}, u32[]{:S(2)}) %all-to-all-start.1) | async-done | bytes 2359328 | tf_op jit(solution)/shard_map/all_to_all | solution.py:35
  204.5 9.7 %reduce-scatter.5.cloned.1.call-done = f32[384,768]{1,0:T(8,128)} async-done(((f32[1536,768]{1,0:T(8,128)}), f32[384,768]{1,0:T(8,128)}) %reduce-scatter.5.cloned.1.call-update) | async-done | bytes 1179664 | tf_op jit(solution)/shard_map/reduce_scatter | solution.py:160
  214.2 2.4 multiply_reduce_fusion.3
  221.2 26.9 %all-gather.3.cloned.1.call-done = bf16[1536,768]{1,0:T(8,128)(2,1)} async-done(((bf16[384,768]{1,0:T(8,128)(2,1)}), bf16[1536,768]{1,0:T(8,128)(2,1)}) %all-gather.3.cloned.1.call-update) | async-done | bytes 2359312 | tf_op jit(solution)/shard_map/all_gather | solution.py:168
  248.1 2.6 convolution_convert_fusion.1
  251.3 5.5 fusion.27
  256.9 7.3 multiply_reduce_fusion
  264.1 11.2 %multiply_convert_fusion = bf16[3,3,512,512]{2,3,1,0:T(8,128)(2,1)} fusion(f32[3,3,512,512]{2,3,1,0:T(8,128)} %get-tuple-element.58, f32[3,3,512,512]{2,3,1,0:T(8,128)} %copy-done.2, f32[3,3,512]{2,1,0:T(4,128)S(1)} %get-tuple-element.57, f32[3,3,512]{2,1,0:T(4,128)S(1)} %log_add_fusion), kind=kLoop, calls=%fused_computation | loop fusion | flops 11796480 | bytes 23629824 | tf_op jit(solution)/shard_map/convert_element_type | solution.py:87
  275.4 4.0 fusion.31
  291.6 4.2 convolution_bitcast_fusion
  295.8 4.9 all-to-all-start.3
  300.8 55.3 %all-to-all-done.3 = f32[4,384,768]{2,1,0:T(8,128)} async-done(((f32[4,384,768]{2,1,0:T(8,128)}), f32[4,384,768]{2,1,0:T(8,128)}, u32[]{:S(2)}, u32[]{:S(2)}) %all-to-all-start.3) | async-done | bytes 4718624 | tf_op jit(solution)/shard_map/all_to_all | solution.py:41
  356.1 3.5 fusion.59
  364.9 6.0 fusion.33
  370.9 7.1 fusion.37
  379.8 3.1 fusion.18
  384.2 45.8 %all_to_all.20 = bf16[4,384,768]{2,1,0:T(8,128)(2,1)S(1)} all-to-all(bf16[4,384,768]{2,1,0:T(8,128)(2,1)S(1)} %broadcast_in_dim.13), channel_id=1, replica_groups=mesh['dp'=32,'tensor'=4] {'tensor'}, dimensions={0} | all-to-all | bytes 4718592 | tf_op jit(solution)/shard_map/all_to_all | solution.py:21
  430.4 158.3 %all-reduce = (f32[768]{0:T(1024)S(1)}, f32[768]{0:T(1024)S(1)}, f32[2,192]{1,0:T(2,128)}, f32[768]{0:T(1024)S(1)}, f32[768]{0:T(1024)S(1)}, /*index=5*/f32[768]{0:T(1024)S(1)}, f32[768]{0:T(1024)}, f32[768]{0:T(1024)S(1)}) all-reduce(f32[768]{0:T(1024)} %get-tuple-element.14, ...), channel_id=1, replica_groups=mesh['dp'=32,'tensor'=4] {'dp'}, use_global_device_ids=true, to_apply=%region_18.0 | all-reduce | flops 5760 | bytes 46080 | tf_op jit(solution)/shard_map/psum | solution.py:197
  588.7 15.3 %all-reduce.2 = (f32[768]{0:T(1024)}, f32[768]{0:T(1024)}, f32[768]{0:T(1024)}, f32[768]{0:T(1024)}, f32[768]{0:T(1024)}, /*index=5*/f32[768]{0:T(1024)}) all-reduce(f32[768]{0:T(1024)S(1)} %get-tuple-element.21, f32[768]{0:T(1024)S(1)} %get-tuple-element.22, ...), channel_id=1, replica_groups=mesh['dp'=32,'tensor'=4] {'tensor'}, use_global_device_ids=true, to_apply=%region_19.0 | all-reduce | flops 4608 | bytes 36864 | tf_op jit(solution)/shard_map/psum | solution.py:214
  604.0 130.2 %all-reduce.5.cloned.1.call-done = (f32[3,768,192]{1,2,0:T(8,128)}, f32[192,768]{1,0:T(8,128)}, f32[768,768]{1,0:T(8,128)}, f32[768,768]{1,0:T(8,128)}) async-done(((f32[3,768,192]{1,2,0:T(8,128)}, f32[192,768]{1,0:T(8,128)}, f32[768,768]{1,0:T(8,128)}, f32[768,768]{1,0:T(8,128)}), (f32[3,768,192]{1,2,0:T(8,128)}, f32[192,768]{1,0:T(8,128)}, f32[768,768]{1,0:T(8,128)}, ...) | async-done | bytes 7077904 | tf_op jit(solution)/shard_map/psum | solution.py:197
  (190 shorter events, 67.4 us)
Async XLA Ops:
  7.2 127.3 %copy-start = (bf16[768,768]{1,0:T(8,128)(2,1)S(1)}, bf16[768,768]{1,0:T(8,128)(2,1)}, u32[]{:S(2)}) copy-start(bf16[768,768]{1,0:T(8,128)(2,1)} %param.30) | copy-start | bytes 3538948
  7.2 84.3 %reduce-scatter.3.cloned.1.call-start = ((), (), s32[]{:S(2)}) async-start(), calls=%async_computation.6 | async-start | bytes 5898240 | tf_op jit(solution)/shard_map/reduce_scatter | solution.py:134
  38.1 55.7 %copy-start.34 = (f32[768]{0:T(1024)S(1)}, f32[768]{0:T(1024)}, u32[]{:S(2)}) copy-start(f32[768]{0:T(1024)} %param.26) | copy-start | bytes 9220
  38.1 55.7 %copy-start.48 = (f32[768]{0:T(1024)S(1)}, f32[768]{0:T(1024)}, u32[]{:S(2)}) copy-start(f32[768]{0:T(1024)} %param.27) | copy-start | bytes 9220
  95.6 34.7 %all-to-all-start = ((bf16[4,384,768]{2,1,0:T(8,128)(2,1)}), bf16[4,384,768]{2,1,0:T(8,128)(2,1)}, u32[]{:S(2)}, u32[]{:S(2)}) async-start(bf16[4,384,768]{2,1,0:T(8,128)(2,1)} %broadcast_in_dim.12), calls=%async_computation.1 | async-start | bytes 4718592 | tf_op jit(solution)/shard_map/all_to_all | solution.py:21
  100.3 113.9 %reduce-scatter.5.cloned.1.call-start = ((), (), s32[]{:S(2)}) async-start(), calls=%async_computation.7 | async-start | bytes 5898240 | tf_op jit(solution)/shard_map/reduce_scatter | solution.py:160
  100.5 57.0 %copy-start.35 = (f32[1536]{0:T(1024)}, f32[1536]{0:T(1024)S(1)}, u32[]{:S(2)}) copy-start(f32[1536]{0:T(1024)S(1)} %maximum_convert_fusion) | copy-start | bytes 18436
  134.5 5.7 copy-start.58
  134.5 7.1 copy-start.51
  152.7 49.6 %all-to-all-start.1 = ((bf16[4,384,768]{2,1,0:T(8,128)(2,1)}), bf16[4,384,768]{2,1,0:T(8,128)(2,1)}, u32[]{:S(2)}, u32[]{:S(2)}) async-start(bf16[4,384,768]{2,1,0:T(8,128)(2,1)} %bitcast.80), calls=%async_computation.2 | async-start | bytes 4718592 | tf_op jit(solution)/shard_map/all_to_all | solution.py:35
  157.5 90.6 %all-gather.3.cloned.1.call-start = ((), (), s32[]{:S(2)}) async-start(), calls=%async_computation.8 | async-start | bytes 2949120 | tf_op jit(solution)/shard_map/all_gather | solution.py:168
  162.0 54.7 %copy-start.49 = (f32[768]{0:T(1024)S(1)}, f32[768]{0:T(1024)}, u32[]{:S(2)}) copy-start(f32[768]{0:T(1024)} %param.31) | copy-start | bytes 9220
  218.1 30.0 %copy-start.27 = (bf16[192,768]{1,0:T(8,128)(2,1)S(1)}, bf16[192,768]{1,0:T(8,128)(2,1)}, u32[]{:S(2)}) copy-start(bf16[192,768]{1,0:T(8,128)(2,1)} %param.24) | copy-start | bytes 884740
  251.3 5.6 copy-start.16
  264.1 11.2 %copy-start.6 = (bf16[3,512,3,64]{1,0,3,2:T(4,128)(2,1)S(1)}, bf16[3,512,3,64]{1,0,3,2:T(4,128)(2,1)}, u32[]{:S(2)}) copy-start(bf16[3,512,3,64]{1,0,3,2:T(4,128)(2,1)} %squeeze.7) | copy-start | bytes 1769476
  283.5 6.8 copy-start.7
  295.8 60.3 %all-to-all-start.3 = ((f32[4,384,768]{2,1,0:T(8,128)}), f32[4,384,768]{2,1,0:T(8,128)}, u32[]{:S(2)}, u32[]{:S(2)}) async-start(f32[4,384,768]{2,1,0:T(8,128)} %convolution_bitcast_fusion), calls=%async_computation.5 | async-start | bytes 9437184 | tf_op jit(solution)/shard_map/all_to_all | solution.py:41
  300.8 303.2 %all-gather.5.cloned.1.call-start = ((), (), s32[]{:S(2)}) async-start(), calls=%async_computation.9 | async-start | bytes 2949120 | tf_op jit(solution)/shard_map/all_gather | solution.py:194
  300.8 58.8 %copy-start.38 = (f32[768]{0:T(1024)S(1)}, f32[768]{0:T(1024)}, u32[]{:S(2)}) copy-start(f32[768]{0:T(1024)} %param.20) | copy-start | bytes 9220
  364.8 6.1 copy-start.22
  364.8 6.1 copy-start.36
  364.9 6.1 copy-start.55
  364.9 369.3 %all-reduce.5.cloned.1.call-start = ((), (), s32[]{:S(2)}) async-start(), calls=%async_computation.10 | async-start | bytes 14155776 | tf_op jit(solution)/shard_map/psum | solution.py:197
  370.9 7.2 copy-start.13
  370.9 7.2 copy-start.50
  370.9 8.6 %copy-start.31 = (bf16[3,1536,192]{1,2,0:T(8,128)(2,1)S(1)}, bf16[3,1536,192]{1,2,0:T(8,128)(2,1)}, u32[]{:S(2)}) copy-start(bf16[3,1536,192]{1,2,0:T(8,128)(2,1)} %copy-done.30) | copy-start | bytes 5308420
  384.1 45.9 %copy-start.8 = (bf16[1,1536,192]{1,2,0:T(8,128)(2,1)S(1)}, bf16[1,1536,192]{1,2,0:T(8,128)(2,1)}, u32[]{:S(2)}) copy-start(bf16[1,1536,192]{1,2,0:T(8,128)(2,1)} %copy-done.7) | copy-start | bytes 1769476
  384.2 46.0 %copy-start.10 = (bf16[1,1536,192]{1,2,0:T(8,128)(2,1)S(1)}, bf16[1,1536,192]{1,2,0:T(8,128)(2,1)}, u32[]{:S(2)}) copy-start(bf16[1,1536,192]{1,2,0:T(8,128)(2,1)} %copy-done.9) | copy-start | bytes 1769476
  384.2 46.2 %copy-start.40 = (f32[768]{0:T(1024)S(1)}, f32[768]{0:T(1024)}, u32[]{:S(2)}) copy-start(f32[768]{0:T(1024)} %get-tuple-element.18) | copy-start | bytes 9220
  384.2 46.2 %copy-start.41 = (f32[768]{0:T(1024)S(1)}, f32[768]{0:T(1024)}, u32[]{:S(2)}) copy-start(f32[768]{0:T(1024)} %get-tuple-element.20) | copy-start | bytes 9220
  384.2 46.2 %copy-start.42 = (f32[768]{0:T(1024)S(1)}, f32[768]{0:T(1024)}, u32[]{:S(2)}) copy-start(f32[768]{0:T(1024)} %get-tuple-element.39) | copy-start | bytes 9220
  384.2 46.2 %copy-start.43 = (f32[768]{0:T(1024)S(1)}, f32[768]{0:T(1024)}, u32[]{:S(2)}) copy-start(f32[768]{0:T(1024)} %get-tuple-element.47) | copy-start | bytes 9220
  (35 other events, 95.8 us)
Sparse Core Ops, SparseCore 0:
  34.3 57.1 reduce-scatter.2
  146.0 68.1 reduce-scatter.4
  221.2 26.7 all-gather.2
  364.9 26.9 all-gather.4
  395.7 338.3 all-reduce.4
where the time goes:
time: 762 us; the launch traced here: 753 us
  waiting for transfers between devices  346 us (45%)
  blocking collectives  219 us (29%)
  matrix products  72.9 us (10%)
  other arithmetic  45 us (6%)
  local copies, waits for them, and re-layouts  39.9 us (5%)
  between operations  15 us (2%)
  starting transfers between devices  14.7 us (2%)
    psum x1, blocking collectives, shards(): lax.psum((grad_w_qkv, grad_b_qv, grad_w_out, grad_w_up, grad_b_up, grad_w...  158 us
    psum x1, waiting for transfers between devices, shards(): lax.psum((grad_w_qkv, grad_b_qv, grad_w_out, grad_w_up, grad_b_up, grad_w...  130 us
    all_to_all x1, waiting for transfers between devices, sum_at_owner(): lax.all_to_all(pieces, axis, split_axis=0, concat_axis=0, tiled=True)  55.3 us
    reduce_scatter x1, waiting for transfers between devices, shards(): lax.psum_scatter(branch, 'tensor', scatter_dimension=0, tiled=True)  53.4 us
    all_to_all x1, blocking collectives, sent_to_all(): return lax.all_to_all(copies, axis, split_axis=0, concat_axis=0, tiled=True)  45.8 us
    all_to_all x1, waiting for transfers between devices, summed_on_arrival(): lax.all_to_all(in_blocks(array, dim, count), axis, 0, 0, tiled=True)  40.4 us
    all_to_all x1, waiting for transfers between devices, sent_to_all(): return lax.all_to_all(copies, axis, split_axis=0, concat_axis=0, tiled=True)  29.8 us
    all_gather x1, waiting for transfers between devices, shards(): lax.all_gather(grad_middle_rows.astype(jnp.bfloat16), 'tensor', axis=0, t...  26.9 us
  transfers between devices with their start and end apart: 8, of which 7 were waited for; matrix products, arithmetic and copies ran while one was open for 5% of the time, Pallas kernels for 0%

commit v1 on v0

v1 whole, which is shorter than its diff:
```python
import functools

import jax
import jax.numpy as jnp
from jax import lax
from jax.experimental import pallas as pl
from jax.experimental.pallas import tpu as pltpu
from jax.sharding import PartitionSpec as P

MESH = pl.DeviceIdType.MESH
BF = jnp.bfloat16
F32 = jnp.float32
D = 768
HD = 64
LEN = 512
HALF = 256
SEQS = 3
ROWS = SEQS * LEN
EPS = 1e-05
SCALE = HD**-0.5
GELU_A = 0.7978845608028654
GELU_B = 0.044715

NN = (((1,), (0,)), ((), ()))
NT = (((1,), (1,)), ((), ()))
TN = (((0,), (0,)), ((), ()))

GAIN1, SHIFT1, GAIN2, SHIFT2, BOUT, BDOWN, BUP, BQV = range(8)


def dot(a, b, dims):
    return lax.dot_general(a, b, dims, preferred_element_type=F32)


def norm_parts(v):
    centred = v - jnp.mean(v, axis=1, keepdims=True)
    r = lax.rsqrt(jnp.mean(centred * centred, axis=1, keepdims=True) + EPS)
    return centred * r, r


def norm_back(v, e, gain):
    n, r = norm_parts(v)
    eg = e * gain
    grad = r * (
        eg
        - jnp.mean(eg, axis=1, keepdims=True)
        - n * jnp.mean(eg * n, axis=1, keepdims=True)
    )
    return grad, n


def col_sum(v):
    return jnp.sum(v, axis=0, keepdims=True)


def head_part(v, h):
    lane = lax.broadcasted_iota(jnp.int32, v.shape, 1)
    return jnp.where((lane >= HD * h) & (lane < HD * h + HD), v, jnp.zeros_like(v))


class Place:
    def __init__(self):
        dp = lax.axis_index("dp")
        self.t = t = lax.axis_index("tensor")
        self.z = dp // 8
        self.yl = (dp // 4) % 2
        self.x = dp % 4
        self.c = t % 2
        self.t_sib = t + 1 - 2 * self.c
        self.t_part = (t + 2) % 4
        self.t_far = (self.t_sib + 2) % 4
        self.sib = (dp, self.t_sib)
        self.part = (dp, self.t_part)
        self.ypeer = (dp + 4 - 8 * self.yl, t)
        self.dp = dp

    def xpeer(self, j):
        return (self.dp - self.x + (self.x + j) % 4, self.t)

    def zpeer(self, j):
        return (((self.z + j) % 4) * 8 + self.dp % 8, self.t)

    def peers(self):
        return (
            [self.sib, self.part, self.ypeer]
            + [self.xpeer(j) for j in (1, 2, 3)]
            + [self.zpeer(j) for j in (1, 2, 3)]
        )


def remote(src, dst, send, recv, device):
    return pltpu.make_async_remote_copy(
        src_ref=src,
        dst_ref=dst,
        send_sem=send,
        recv_sem=recv,
        device_id=device,
        device_id_type=MESH,
    )


class Reduction:
    def __init__(self, at, stg, r1, r2, ry, send, recv, free):
        self.at, self.stg, self.r1, self.r2, self.ry = at, stg, r1, r2, ry
        self.send, self.recv, self.free = send, recv, free
        self.big = stg.shape[1] // 4
        self.small = stg.shape[1] // 16

    def axes(self, h):
        at = self.at
        if h == 0:
            return at.x, at.z, at.xpeer, at.zpeer
        return at.z, at.x, at.zpeer, at.xpeer

    def block(self, h, first):
        return self.stg.at[h, pl.ds(pl.multiple_of(first * self.big, self.big), self.big)]

    def part(self, h, first, second):
        start = pl.multiple_of(first * self.big + second * self.small, self.small)
        return self.stg.at[h, pl.ds(start, self.small)]

    def copy(self, h, step, src, dst, device):
        return remote(src, dst, self.send.at[h, step], self.recv.at[h, step], device)

    def out1(self, h, j):
        first, _, peer, _ = self.axes(h)
        return self.copy(h, j - 1, self.block(h, (first + j) % 4), self.r1.at[h, j - 1], peer(j))

    def out2(self, h, j):
        first, second, _, peer = self.axes(h)
        return self.copy(
            h, 2 + j, self.part(h, first, (second + j) % 4), self.r2.at[h, j - 1], peer(j)
        )

    def outy(self, h):
        first, second, _, _ = self.axes(h)
        return self.copy(h, 6, self.part(h, first, second), self.ry.at[h], self.at.ypeer)

    def back2(self, h, j, arriving=False):
        first, second, _, peer = self.axes(h)
        own = self.part(h, first, (second + 4 - j) % 4 if arriving else second)
        return self.copy(h, 6 + j, own, own, peer(j))

    def back1(self, h, j, arriving=False):
        first, _, peer, _ = self.axes(h)
        own = self.block(h, (first + 4 - j) % 4 if arriving else first)
        return self.copy(h, 9 + j, own, own, peer(j))

    def give_back(self, h, stage):
        peer = self.axes(h)[2 + stage]
        for j in (1, 2, 3):
            (self.out1 if stage == 0 else self.out2)(h, j).wait_send()
        for j in (1, 2, 3):
            pl.semaphore_signal(
                self.free.at[h, stage], inc=1, device_id=peer(j), device_id_type=MESH
            )

    def start(self):
        for h in (0, 1):
            for j in (1, 2, 3):
                self.out1(h, j).start()

    def second(self):
        for h in (0, 1):
            for j in (1, 2, 3):
                self.out1(h, j).wait_recv()
            own = self.block(h, self.axes(h)[0])
            total = own[...].astype(F32)
            for j in (0, 1, 2):
                total = total + self.r1[h, j].astype(F32)
            own[...] = total.astype(BF)
            for j in (1, 2, 3):
                self.out2(h, j).start()
            self.give_back(h, 0)

    def third(self):
        for h in (0, 1):
            for j in (1, 2, 3):
                self.out2(h, j).wait_recv()
            first, second, _, _ = self.axes(h)
            own = self.part(h, first, second)
            total = own[...].astype(F32)
            for j in (0, 1, 2):
                total = total + self.r2[h, j].astype(F32)
            own[...] = total.astype(BF)
            self.outy(h).start()
            self.give_back(h, 1)

    def fourth(self):
        for h in (0, 1):
            self.outy(h).wait()
            first, second, _, _ = self.axes(h)
            own = self.part(h, first, second)
            own[...] = (own[...].astype(F32) + self.ry[h].astype(F32)).astype(BF)
            pl.semaphore_wait(self.free.at[h, 1], 3)
            for j in (1, 2, 3):
                self.back2(h, j).start()

    def fifth(self):
        for h in (0, 1):
            for j in (1, 2, 3):
                self.back2(h, j, True).wait_recv()
            pl.semaphore_wait(self.free.at[h, 0], 3)
            for j in (1, 2, 3):
                self.back1(h, j).start()

    def finish(self):
        for h in (0, 1):
            for j in (1, 2, 3):
                self.back1(h, j, True).wait_recv()

    def drain(self):
        for h in (0, 1):
            for j in (1, 2, 3):
                self.back2(h, j).wait_send()
                self.back1(h, j).wait_send()


def kernel(
    comm,
    x_hbm,
    cot_hbm,
    wqkv_hbm,
    wout_hbm,
    wup_hbm,
    wdown_hbm,
    weight_ref,
    bqv_ref,
    vec_ref,
    bup_ref,
    out_hbm,
    gin_hbm,
    g0_hbm,
    g1_hbm,
    small_ref,
    x_ref,
    u_ref,
    wqkv,
    wof,
    wup,
    wdown,
    n1,
    q8,
    keys,
    vals,
    att,
    lse,
    mid,
    gmid,
    nt2,
    actt,
    ghid,
    own_a,
    own_b,
    s1,
    r1,
    s2,
    r2,
    mlow,
    gp,
    sc,
    pr,
    ds,
    stg0,
    stg1,
    b0r1,
    b0r2,
    b0ry,
    b1r1,
    b1r2,
    b1ry,
    sm,
    smc,
    smx,
    smz,
    smy,
    in_sem,
    out_sem,
    a_send,
    a_recv,
    t_send,
    t_recv,
    d0_send,
    d0_recv,
    d0_free,
    d1_send,
    d1_recv,
    d1_free,
    m_send,
    m_recv,
):
    at = Place()
    c = at.c
    if not comm:
        c = 0
    gin = ghid
    gpt = nt2.at[0:576]
    res = u_ref

    def rows_of(s, half=None):
        if half is None:
            return pl.ds(pl.multiple_of(s * LEN, LEN), LEN)
        return pl.ds(pl.multiple_of(s * LEN + half * HALF, HALF), HALF)

    def wout_block(t):
        return wof.at[pl.ds(pl.multiple_of(t * 192, 192), 192)]

    def att_block(s, t):
        return att.at[s, pl.ds(pl.multiple_of(t * 192, 192), 192)]

    def load(i, src, dst):
        return pltpu.make_async_copy(src, dst, in_sem.at[i])

    def load_x(s):
        return load(s, x_hbm.at[rows_of(s)], x_ref.at[rows_of(s)])

    load_wqkv = load(3, wqkv_hbm, wqkv)
    load_wout = load(4, wout_hbm, wout_block(at.t))
    load_cot = load(5, cot_hbm, u_ref)
    load_up = load(6, wup_hbm, wup)
    load_down = load(7, wdown_hbm, wdown)
    load_wout.start()
    load_x(0).start()
    load_wqkv.start()
    load_x(1).start()
    load_x(2).start()
    load_cot.start()
    load_up.start()
    load_down.start()

    sm[...] = jnp.zeros_like(sm)
    if comm:
        barrier = pltpu.get_barrier_semaphore()
        peers = at.peers()
        for peer in peers:
            pl.semaphore_signal(barrier, inc=1, device_id=peer, device_id_type=MESH)
        pl.semaphore_wait(barrier, len(peers))

    def gather_copies(i, block):
        def copy(kind, t, device):
            ref = block(t)
            return remote(ref, ref, a_send.at[i, kind], a_recv.at[i, kind], device)

        return copy

    def gather_start(i, block):
        if comm:
            copy = gather_copies(i, block)
            copy(1, at.t, at.part).start()
            copy(0, at.t, at.sib).start()

    def gather_forward(i, block):
        if comm:
            copy = gather_copies(i, block)
            copy(1, at.t_part, at.part).wait_recv()
            copy(2, at.t_part, at.sib).start()

    def gather_wait(i, block):
        if comm:
            copy = gather_copies(i, block)
            copy(0, at.t_sib, at.sib).wait_recv()
            copy(2, at.t_far, at.sib).wait_recv()

    def gather_drain(i, block):
        if comm:
            copy = gather_copies(i, block)
            copy(0, at.t, at.sib).wait_send()
            copy(1, at.t, at.part).wait_send()
            copy(2, at.t_part, at.sib).wait_send()

    def att_of(s):
        return functools.partial(att_block, s)

    load_wout.wait()
    gather_start(3, wout_block)

    def room(k):
        return k % 2

    def first_copy(k, s):
        i = room(k)
        return remote(s1.at[i, s], r1.at[i, s], t_send.at[k, s, 0], t_recv.at[k, s, 0], at.sib)

    def second_copy(k, s):
        return remote(
            s2.at[room(k), s], r2.at[k, s], t_send.at[k, s, 1], t_recv.at[k, s, 1], at.part
        )

    def third_copy(k, s, target, arriving=False):
        ref = target.at[rows_of(s, 1 - c if arriving else c)]
        return remote(ref, ref, t_send.at[k, s, 2], t_recv.at[k, s, 2], at.sib)

    def chip_sum(k, s, own):
        if comm:
            first_copy(k, s).wait()
        total = own[s] + r1[room(k), s].astype(F32)
        s2[room(k), s] = total.astype(BF)
        if comm:
            second_copy(k, s).start()

    def group_sum(k, s):
        if comm:
            second_copy(k, s).wait()
        return s2[room(k), s].astype(F32) + r2[k, s].astype(F32)

    def share(k, s, target):
        if comm:
            third_copy(k, s, target).start()

    def share_wait(k, s, target):
        if comm:
            third_copy(k, s, target, True).wait_recv()

    def share_drain(k, s, target):
        if comm:
            third_copy(k, s, target).wait_send()

    gain1, shift1 = vec_ref[0:1, :], vec_ref[1:2, :]
    gain2, shift2 = vec_ref[2:3, :], vec_ref[3:4, :]
    b_out, b_down = vec_ref[4:5, :], vec_ref[5:6, :]

    def add_small(row, value):
        sm[row : row + 1, :] += value

    def attend(s, _):
        load_x(s).wait()

        @pl.when(s == 0)
        def _():
            load_wqkv.wait()

        rows = rows_of(s)
        n, _r = norm_parts(x_ref[rows, :].astype(F32))
        normed = (n * gain1 + shift1).astype(BF)
        n1[rows, :] = normed
        q = (dot(normed, wqkv[0], NT) + bqv_ref[0:1, :]).astype(BF) * SCALE
        q8[s] = q
        k = dot(normed, wqkv[1], NT).astype(BF)
        keys[s] = k
        v = (dot(normed, wqkv[2], NT) + bqv_ref[1:2, :]).astype(BF)
        vals[s] = v
        vt = v.T
        block = att_block(s, at.t if comm else 0)
        for h in range(3):
            sc[...] = dot(head_part(k, h), q, NT)
            for part in range(4):
                cols = slice(part * 128, part * 128 + 128)
                scores = sc[:, cols]
                top = jnp.max(scores, axis=0, keepdims=True)
                e = jnp.exp(scores - top)
                total = col_sum(e)
                lse[3 * s + h, :, cols] = top + jnp.log(total)
                pr[:, cols] = (e * (1.0 / total)).astype(BF)
            mixed = dot(vt[HD * h : HD * h + HD], pr[...], NN)
            block[HD * h : HD * h + HD, :] = mixed.astype(BF)
        gather_start(s, att_of(s))

        @pl.when(s == 0)
        def _():
            gather_forward(3, wout_block)

        @pl.when(s > 0)
        def _():
            gather_forward(s - 1, att_of(s - 1))

        return 0

    lax.fori_loop(0, SEQS, attend, 0)

    load_cot.wait()

    def weigh(i, _):
        rows = pl.ds(pl.multiple_of(i * HALF, HALF), HALF)
        same = lax.broadcasted_iota(jnp.int32, (HALF, HALF), 0) == lax.broadcasted_iota(
            jnp.int32, (HALF, HALF), 1
        )
        diagonal = jnp.where(same, weight_ref[pl.ds(i, 1), :], 0.0).astype(BF)
        u_ref[rows, :] = dot(diagonal, u_ref[rows, :], NN).astype(BF)
        return 0

    lax.fori_loop(0, 2 * SEQS, weigh, 0)

    load_up.wait()
    load_down.wait()
    gather_wait(3, wout_block)

    def feed(s, _):
        gather_wait(s, att_of(s))
        for own in (False, True):
            half = c if own else 1 - c
            rows = rows_of(s, half)
            cols = pl.ds(pl.multiple_of(half * HALF, HALF), HALF)
            middle = x_ref[rows, :].astype(F32) + dot(att[s, :, cols], wof[...], TN) + b_out
            if own:
                mid[s] = middle
            n, _r = norm_parts(middle)
            normed = (n * gain2 + shift2).astype(BF)
            nt2[:, rows] = normed.T
            v = dot(normed, wup[...], NN) + bup_ref[...]
            back = dot(u_ref[rows, :], wdown[...], NT)
            square = v * v
            th = jnp.tanh(GELU_A * (v + GELU_B * square * v))
            cdf = 0.5 * (1.0 + th)
            act = (v * cdf).astype(BF)
            slope = cdf + (0.5 * GELU_A) * v * (1.0 - th * th) * (1.0 + (3.0 * GELU_B) * square)
            actt[:, rows] = act.T
            grad = back * slope
            add_small(BUP, col_sum(grad))
            grad = grad.astype(BF)
            ghid[rows, :] = grad
            normed_back = dot(grad, wup[...], NT)
            down = dot(act, wdown[...], NN)
            if own:
                own_a[s] = normed_back
                own_b[s] = down
            else:
                s1[0, s] = normed_back.astype(BF)
                s1[1, s] = down.astype(BF)
                if comm:
                    first_copy(0, s).start()
                    first_copy(1, s).start()
        chip_sum(0, s, own_a)

        @pl.when(s == 0)
        def _():
            gather_forward(2, att_of(2))

        return 0

    lax.fori_loop(0, SEQS, feed, 0)
    chip_sum(1, 0, own_b)

    def middle_back(s):
        e = group_sum(0, s)
        grad, n = norm_back(mid[s], e, gain2)
        add_small(GAIN2, col_sum(e * n))
        add_small(SHIFT2, col_sum(e))
        up = u_ref[rows_of(s, c), :].astype(F32)
        grad = up + grad
        add_small(BOUT, col_sum(grad))
        add_small(BDOWN, col_sum(up))
        gmid[s] = grad
        mlow[rows_of(s, c), :] = grad.astype(BF)
        share(0, s, mlow)

    middle_back(0)

    d0 = Reduction(at, stg0, b0r1, b0r2, b0ry, d0_send, d0_recv, d0_free)
    d1 = Reduction(at, stg1, b1r1, b1r2, b1ry, d1_send, d1_recv, d1_free)

    def stage(stg, start, count, value):
        where = pl.ds(start, count)
        stg[0, where, :] = value[:, :384].astype(BF)
        stg[1, where, :] = value[:, 384:].astype(BF)

    def up_grads(i, _):
        start = pl.multiple_of(i * HALF, HALF)
        some = pl.ds(start, HALF)
        stage(stg0, start, HALF, dot(nt2[some, :], ghid[...], NN))
        return 0

    def down_grads(i, _):
        start = pl.multiple_of(i * HALF, HALF)
        some = pl.ds(start, HALF)
        stage(stg0, D + start, HALF, dot(actt[some, :], u_ref[...], NN))
        return 0

    lax.fori_loop(0, 3, up_grads, 0)
    lax.fori_loop(0, 3, down_grads, 0)
    if comm:
        d0.start()

    def attend_back(s):
        @pl.when(s < SEQS - 1)
        def _():
            middle_back(s + 1)

        share_wait(0, s, mlow)
        rows = rows_of(s)
        mixed = dot(mlow[rows, :], wout_block(at.t if comm else 0)[...], NT).astype(BF)
        q, k, v = q8[s], keys[s], vals[s]
        kt = k.T
        grad_k = jnp.zeros((LEN, 192), F32)
        grad_v = jnp.zeros((LEN, 192), F32)
        for h in range(3):
            sc[...] = dot(head_part(k, h), q, NT)
            back = dot(head_part(v, h), mixed, NT)
            some = slice(HD * h, HD * h + HD)
            for part in range(4):
                cols = slice(part * 128, part * 128 + 128)
                p = jnp.exp(sc[:, cols] - lse[3 * s + h, :, cols])
                pr[:, cols] = p.astype(BF)
                gp_part = back[:, cols]
                total = col_sum(gp_part * p)
                ds[:, cols] = (p * (gp_part - total)).astype(BF)
            grad_v += dot(pr[...], head_part(mixed, h), NN)
            grad_k += dot(ds[...], head_part(q, h), NN)
            gpt[some, rows] = (dot(kt[some], ds[...], NN) * SCALE).astype(BF)
        gp[0] = gpt[0:192, rows].T
        gp[1] = grad_k.astype(BF)
        gp[2] = grad_v.astype(BF)
        gpt[192:384, rows] = gp[1].T
        gpt[384:576, rows] = gp[2].T
        sm[BQV : BQV + 1, 0:192] += col_sum(gp[0].astype(F32))
        sm[BQV : BQV + 1, 256:448] += col_sum(gp[2].astype(F32))
        for own in (False, True):
            half = c if own else 1 - c
            some = pl.ds(pl.multiple_of(half * HALF, HALF), HALF)
            total = dot(gp[0, some, :], wqkv[0], NN)
            total += dot(gp[1, some, :], wqkv[1], NN)
            total += dot(gp[2, some, :], wqkv[2], NN)
            if own:
                own_a[s] = total
            else:
                s1[0, s] = total.astype(BF)
                if comm:
                    first_copy(2, s).start()
        chip_sum(2, s, own_a)

    def reduce_step(name, which):
        if comm:
            getattr(which, name)()

    def attend_back_all():
        def step(s, _):
            attend_back(s)

            @pl.when(s == 0)
            def _():
                reduce_step("second", d0)

            @pl.when(s == 1)
            def _():
                reduce_step("third", d0)

            @pl.when(s == 2)
            def _():
                reduce_step("fourth", d0)

            return 0

        lax.fori_loop(0, SEQS, step, 0)

    attend_back_all()
    chip_sum(1, 1, own_b)
    chip_sum(1, 2, own_b)

    def qkv_grads(i, _):
        start = pl.multiple_of(i * 192, 192)
        stage(stg1, start, 192, dot(gpt[pl.ds(start, 192), :], n1[...], NN))
        return 0

    lax.fori_loop(0, 3, qkv_grads, 0)
    total = jnp.zeros((192, D), F32)
    for s in range(SEQS):
        total += dot(att_block(s, at.t if comm else 0)[...], mlow[rows_of(s), :], NN)
    stage(stg1, 576, 192, total)
    if comm:
        d1.start()

    def input_back(s):
        e = group_sum(2, s)
        rows = rows_of(s, c)
        grad, n = norm_back(x_ref[rows, :].astype(F32), e, gain1)
        add_small(GAIN1, col_sum(e * n))
        add_small(SHIFT1, col_sum(e))
        gin[rows, :] = (gmid[s] + grad).astype(BF)
        share(2, s, gin)

    def output_rows(s):
        rows = rows_of(s, c)
        res[rows, :] = (mid[s] + group_sum(1, s) + b_down).astype(BF)
        share(1, s, res)

    def store(i, src, dst):
        return pltpu.make_async_copy(src, dst, out_sem.at[i])

    def store_rows(k, s):
        src, dst = (res, out_hbm) if k == 1 else (gin, gin_hbm)
        rows = rows_of(s)
        return store(s if k == 1 else SEQS + s, src.at[rows], dst.at[rows])

    def finish_rows(k, s):
        share_wait(k, s, res if k == 1 else gin)
        store_rows(k, s).start()

    def small_copy(i, slots, slot, device):
        ref = slots.at[slot]
        return remote(ref, ref, m_send.at[i], m_recv.at[i], device)

    def small_chip():
        smc[c] = sm[...]
        small_copy(0, smc, c, at.sib).start()

    def small_x():
        small_copy(0, smc, 1 - c, at.sib).wait_recv()
        row = lax.broadcasted_iota(jnp.int32, (8, D), 0)
        smx[at.x] = jnp.where(row < BUP, smc[0] + smc[1], smc[c])
        for j in (1, 2, 3):
            small_copy(j, smx, at.x, at.xpeer(j)).start()

    def small_z():
        for j in (1, 2, 3):
            small_copy(j, smx, (at.x + 4 - j) % 4, at.xpeer(j)).wait_recv()
        smz[at.z] = (smx[0] + smx[1]) + (smx[2] + smx[3])
        for j in (1, 2, 3):
            small_copy(3 + j, smz, at.z, at.zpeer(j)).start()

    def small_y():
        for j in (1, 2, 3):
            small_copy(3 + j, smz, (at.z + 4 - j) % 4, at.zpeer(j)).wait_recv()
        smy[at.yl] = (smz[0] + smz[1]) + (smz[2] + smz[3])
        small_copy(7, smy, at.yl, at.ypeer).start()

    def small_end():
        small_copy(7, smy, 1 - at.yl, at.ypeer).wait_recv()
        small_ref[...] = smy[0] + smy[1]

    def small_drain():
        small_copy(0, smc, c, at.sib).wait_send()
        for j in (1, 2, 3):
            small_copy(j, smx, at.x, at.xpeer(j)).wait_send()
            small_copy(3 + j, smz, at.z, at.zpeer(j)).wait_send()
        small_copy(7, smy, at.yl, at.ypeer).wait_send()

    store_g0 = store(2 * SEQS, stg0, g0_hbm)
    store_g1 = store(2 * SEQS + 1, stg1, g1_hbm)

    output_rows(0)
    input_back(0)
    reduce_step("fifth", d0)
    finish_rows(1, 0)
    input_back(1)
    finish_rows(2, 0)
    reduce_step("second", d1)
    input_back(2)
    finish_rows(2, 1)
    if comm:
        small_chip()
    reduce_step("third", d1)
    if comm:
        small_x()
    reduce_step("fourth", d1)
    output_rows(1)
    finish_rows(2, 2)
    if comm:
        small_z()
    reduce_step("fifth", d1)
    finish_rows(1, 1)
    reduce_step("finish", d0)
    store_g0.start()
    if comm:
        small_y()
    output_rows(2)
    if comm:
        small_end()
    else:
        small_ref[...] = sm[...]
    finish_rows(1, 2)
    reduce_step("finish", d1)
    store_g1.start()

    if comm:
        for s in range(SEQS):
            gather_drain(s, att_of(s))
            share_drain(0, s, mlow)
            share_drain(1, s, res)
            share_drain(2, s, gin)
        gather_drain(3, wout_block)
        d0.drain()
        d1.drain()
        small_drain()
    for s in range(SEQS):
        store_rows(1, s).wait()
        store_rows(2, s).wait()
    store_g0.wait()
    store_g1.wait()


def layer(comm, x, cot, wqkv_t, wout, wup, wdown, weight, bqv, vecs, bup):
    half = (SEQS, HALF, D)
    dma = pltpu.SemaphoreType.DMA
    scratch = [
        pltpu.VMEM((ROWS, D), BF),
        pltpu.VMEM((ROWS, D), BF),
        pltpu.VMEM((3, 192, D), BF),
        pltpu.VMEM((D, D), BF),
        pltpu.VMEM((D, D), BF),
        pltpu.VMEM((D, D), BF),
        pltpu.VMEM((ROWS, D), BF),
        pltpu.VMEM((SEQS, LEN, 192), BF),
        pltpu.VMEM((SEQS, LEN, 192), BF),
        pltpu.VMEM((SEQS, LEN, 192), BF),
        pltpu.VMEM((SEQS, D, LEN), BF),
        pltpu.VMEM((3 * SEQS, 1, LEN), F32),
        pltpu.VMEM(half, F32),
        pltpu.VMEM(half, F32),
        pltpu.VMEM((D, ROWS), BF),
        pltpu.VMEM((D, ROWS), BF),
        pltpu.VMEM((ROWS, D), BF),
        pltpu.VMEM(half, F32),
        pltpu.VMEM(half, F32),
        pltpu.VMEM((2, *half), BF),
        pltpu.VMEM((2, *half), BF),
        pltpu.VMEM((2, *half), BF),
        pltpu.VMEM((3, *half), BF),
        pltpu.VMEM((ROWS, D), BF),
        pltpu.VMEM((3, LEN, 192), BF),
        pltpu.VMEM((LEN, LEN), F32),
        pltpu.VMEM((LEN, LEN), BF),
        pltpu.VMEM((LEN, LEN), BF),
        pltpu.VMEM((2, 2 * D, 384), BF),
        pltpu.VMEM((2, D, 384), BF),
        pltpu.VMEM((2, 3, 384, 384), BF),
        pltpu.VMEM((2, 3, 96, 384), BF),
        pltpu.VMEM((2, 96, 384), BF),
        pltpu.VMEM((2, 3, 192, 384), BF),
        pltpu.VMEM((2, 3, 48, 384), BF),
        pltpu.VMEM((2, 48, 384), BF),
        pltpu.VMEM((8, D), F32),
        pltpu.VMEM((2, 8, D), F32),
        pltpu.VMEM((4, 8, D), F32),
        pltpu.VMEM((4, 8, D), F32),
        pltpu.VMEM((2, 8, D), F32),
        dma((8,)),
        dma((2 * SEQS + 2,)),
        dma((SEQS + 1, 3)),
        dma((SEQS + 1, 3)),
        dma((3, SEQS, 3)),
        dma((3, SEQS, 3)),
        dma((2, 13)),
        dma((2, 13)),
        pltpu.SemaphoreType.REGULAR((2, 2)),
        dma((2, 13)),
        dma((2, 13)),
        pltpu.SemaphoreType.REGULAR((2, 2)),
        dma((8,)),
        dma((8,)),
    ]
    anywhere = pl.BlockSpec(memory_space=pl.ANY)
    vmem = pl.BlockSpec(memory_space=pltpu.VMEM)
    return pl.pallas_call(
        functools.partial(kernel, comm),
        out_shape=(
            jax.ShapeDtypeStruct((ROWS, D), BF),
            jax.ShapeDtypeStruct((ROWS, D), BF),
            jax.ShapeDtypeStruct((2, 2 * D, 384), BF),
            jax.ShapeDtypeStruct((2, D, 384), BF),
            jax.ShapeDtypeStruct((8, D), F32),
        ),
        in_specs=[anywhere] * 6 + [vmem] * 4,
        out_specs=(anywhere, anywhere, anywhere, anywhere, vmem),
        scratch_shapes=scratch,
        compiler_params=pltpu.CompilerParams(
            collective_id=0 if comm else None,
            has_side_effects=True,
            vmem_limit_bytes=62 * 2**20,
        ),
        cost_estimate=pl.CostEstimate(
            flops=20 * 10**9, bytes_accessed=20 * 10**6, transcendentals=10**7
        ),
        name="layer",
    )(x, cot, wqkv_t, wout, wup, wdown, weight, bqv, vecs, bup)


def shards(
    layer_input,
    flags,
    loss_mask,
    cotangent,
    gain_one,
    shift_one,
    w_qkv,
    b_qv,
    w_out,
    b_out,
    gain_two,
    shift_two,
    w_up,
    b_up,
    w_down,
    b_down,
    comm=True,
):
    weight = jnp.maximum(flags, loss_mask).astype(F32).reshape(2 * SEQS, HALF)
    vecs = jnp.stack([gain_one, shift_one, gain_two, shift_two, b_out, b_down])
    out, gin, g0, g1, small = layer(
        comm,
        layer_input,
        cotangent,
        w_qkv.transpose(0, 2, 1),
        w_out,
        w_up,
        w_down,
        weight,
        b_qv,
        vecs,
        b_up.reshape(1, D),
    )
    g0 = jnp.concatenate([g0[0], g0[1]], axis=1).astype(F32)
    g1 = jnp.concatenate([g1[0], g1[1]], axis=1).astype(F32)
    return (
        out,
        gin,
        small[GAIN1],
        small[SHIFT1],
        g1[:576].reshape(3, 192, D).transpose(0, 2, 1),
        jnp.stack([small[BQV, 0:192], small[BQV, 256:448]]),
        g1[576:],
        small[BOUT],
        small[GAIN2],
        small[SHIFT2],
        g0[:D],
        small[BUP],
        g0[D:],
        small[BDOWN],
    )


def solution(mesh):
    in_specs = (
        P("dp", None),
        P("dp"),
        P("dp"),
        P("dp", None),
        P(),
        P(),
        P(None, None, "tensor"),
        P(None, "tensor"),
        P("tensor", None),
        P(),
        P(),
        P(),
        P(None, "tensor"),
        P("tensor"),
        P("tensor", None),
        P(),
    )
    out_specs = (
        P("dp", None),
        P("dp", None),
        P(),
        P(),
        P(None, None, "tensor"),
        P(None, "tensor"),
        P("tensor", None),
        P(),
        P(),
        P(),
        P(None, "tensor"),
        P("tensor"),
        P("tensor", None),
        P(),
    )
    return jax.shard_map(shards, mesh=mesh, in_specs=in_specs, out_specs=out_specs, check_vma=False)
```

time: 762 us -> 152 us (0.20); the launches traced: 753 us -> 152 us
  waiting for transfers between devices: 346 us -> 0 us
  blocking collectives: 219 us -> 0 us
  Pallas kernels: 0 us -> 131 us
  matrix products: 72.9 us -> 0 us
  other arithmetic: 45 us -> 2.65 us
  local copies, waits for them, and re-layouts: 39.9 us -> 17 us
  starting transfers between devices: 14.7 us -> 0 us
  between operations: 15 us -> 0.71 us
    psum x2 -> x0, blocking collectives: 174 us -> none  [the longest x1 158 us: shards(): lax.psum((grad_w_qkv, grad_b_qv, grad_w_out, grad_w_up, grad_b_up, grad_w...]
    pallas_call x0 -> x1, Pallas kernels: none -> 131 us  [layer(): pl.pallas_call(functools.partial(kernel, comm), out_shape=(jax.ShapeDtype...]
    psum x1 -> x0, waiting for transfers between devices: 130 us -> none  [shards(): lax.psum((grad_w_qkv, grad_b_qv, grad_w_out, grad_w_up, grad_b_up, grad_w...]
    all_to_all x3 -> x0, waiting for transfers between devices: 125 us -> none  [the longest x1 55.3 us: sum_at_owner(): lax.all_to_all(pieces, axis, split_axis=0, concat_axis=0, tiled=True)]
    dot_general x17 -> x0, matrix products: 71.1 us -> none  [the longest x1 7.25 us: attend_back(): jnp.einsum('slhe,smhe->shlm', grad_mixed, values_all, preferred_element_t...]
    reduce_scatter x2 -> x0, waiting for transfers between devices: 63.1 us -> none  [the longest x1 53.4 us: shards(): lax.psum_scatter(branch, 'tensor', scatter_dimension=0, tiled=True)]
    all_to_all x1 -> x0, blocking collectives: 45.8 us -> none  [sent_to_all(): return lax.all_to_all(copies, axis, split_axis=0, concat_axis=0, tiled=True)]
    all_gather x2 -> x0, waiting for transfers between devices: 26.9 us -> none  [the longest x1 26.9 us: shards(): lax.all_gather(grad_middle_rows.astype(jnp.bfloat16), 'tensor', axis=0, t...]
  transfers between devices with their start and end apart: 8 -> 0, of which waited for: 7 -> 0; matrix products, arithmetic and copies ran while one was open for 5% -> 0% of each run, Pallas kernels for 0% -> 0%
where the time goes in v1:
time: 152 us
  Pallas kernels  131 us (86%)
  local copies, waits for them, and re-layouts  17 us (11%)
  other arithmetic  2.65 us (2%)
    pallas_call x1, Pallas kernels, layer(): pl.pallas_call(functools.partial(kernel, comm), out_shape=(jax.ShapeDtype...  131 us
    another operation x7, local copies, waits for them, and re-layouts, shards(): vecs = jnp.stack([gain_one, shift_one, gain_two, shift_two, b_out, b_down])  4.77 us
    unnamed x10, local copies, waits for them, and re-layouts  4.32 us

profile of v1, /device:TPU:0, one launch (start us, length us, event | category | flops | bytes accessed | tf_op | source)
XLA Modules:
  0.0 151.6 jit_solution(5920584491543891676)
XLA Ops:
  0.6 0.7 stack.24
  1.3 0.7 stack.25
  2.0 0.7 stack.26
  2.7 0.7 stack.27
  3.4 0.7 stack.28
  4.1 0.7 stack.29
  4.8 0.6 stack.30.vec_ref
  5.4 0.7 maximum_convert_fusion.3
  6.1 0.6 reshape.37.weight_ref
  6.7 1.3 reshape.38.bup_ref
  8.0 131.2 %layer.1 = (bf16[1536,768]{1,0:T(8,128)(2,1)}, bf16[1536,768]{1,0:T(8,128)(2,1)}, bf16[2,1536,384]{2,1,0:T(8,128)(2,1)}, bf16[2,768,384]{2,1,0:T(8,128)(2,1)}, f32[8,768]{1,0:T(8,128)}) custom-call(bf16[1536,768]{1,0:T(8,128)(2,1)} %x_hbm.1, bf16[1536,768]{1,0:T(8,128)(2,1)} %cot_hbm.1, bf16[3,192,768]{2,1,0:T(8,128)(2,1)} %bitcast.13, ...), custom_call_target="tpu_custom_call" | custom-call | flops 20000000000 | bytes 20000000 | tf_op jit(solution)/shard_map/layer/pallas_call | solution.py:842
  139.2 1.4 slice_bitcast_fusion.3
  140.6 0.9 maximum_convert_fusion.2
  141.4 0.2 maximum_convert_fusion.1
  141.6 0.0 copy-start.3
  141.6 0.0 copy-start.2
  141.6 1.3 slice.68
  143.0 0.0 copy-done.3
  143.0 0.6 pad_maximum_fusion
  143.5 0.4 copy-done.2
  143.9 0.2 slice_bitcast_fusion.1
  144.2 0.3 maximum_convert_fusion
  144.5 0.0 copy-start.1
  144.5 2.5 %fusion = (f32[768,768]{1,0:T(8,128)}, f32[768,768]{1,0:T(8,128)}) fusion(f32[1536,768]{1,0:T(8,128)S(1)} %maximum_convert_fusion), kind=kLoop, calls=%fused_computation.16 | loop fusion | bytes 9437184 | tf_op jit(solution)/shard_map/slice | solution.py:915
  147.0 0.7 slice_reduce_fusion
  147.7 0.0 copy-done.1
  147.7 0.0 copy-start
  147.7 1.4 copy.32
  149.1 1.1 copy-done
  150.2 1.4 copy.33
  (1 shorter events, 0.0 us)
Async XLA Ops:
  141.6 1.3 copy-start.3
  141.6 2.3 %copy-start.2 = (bf16[2,1536,384]{2,1,0:T(8,128)(2,1)S(1)}, bf16[2,1536,384]{2,1,0:T(8,128)(2,1)}, u32[]{:S(2)}) copy-start(bf16[2,1536,384]{2,1,0:T(8,128)(2,1)} %get-tuple-element.23) | copy-start | bytes 7077892
  144.5 3.2 %copy-start.1 = (bf16[1536,768]{1,0:T(8,128)(2,1)S(1)}, bf16[1536,768]{1,0:T(8,128)(2,1)}, u32[]{:S(2)}) copy-start(bf16[1536,768]{1,0:T(8,128)(2,1)} %get-tuple-element.53) | copy-start | bytes 7077892
  147.7 2.5 %copy-start = (bf16[1536,768]{1,0:T(8,128)(2,1)S(1)}, bf16[1536,768]{1,0:T(8,128)(2,1)}, u32[]{:S(2)}) copy-start(bf16[1536,768]{1,0:T(8,128)(2,1)} %get-tuple-element.54) | copy-start | bytes 7077892

commit v2 on v1

v2 whole, which is shorter than its diff:
```python
import functools

import jax
import jax.numpy as jnp
from jax import lax
from jax.experimental import pallas as pl
from jax.experimental.pallas import tpu as pltpu
from jax.sharding import PartitionSpec as P

MESH = pl.DeviceIdType.MESH
BF = jnp.bfloat16
F32 = jnp.float32
D = 768
HD = 64
LEN = 512
HALF = 256
QUART = 128
SEQS = 3
ROWS = SEQS * LEN
EPS = 1e-05
SCALE = HD**-0.5
GELU_A = 0.7978845608028654
GELU_B = 0.044715

NN = (((1,), (0,)), ((), ()))
NT = (((1,), (1,)), ((), ()))
TN = (((0,), (0,)), ((), ()))

GAIN1, SHIFT1, GAIN2, SHIFT2, BOUT, BDOWN, BUP, BQV = range(8)


def dot(a, b, dims):
    return lax.dot_general(a, b, dims, preferred_element_type=F32)


def norm_parts(v):
    centred = v - jnp.mean(v, axis=1, keepdims=True)
    r = lax.rsqrt(jnp.mean(centred * centred, axis=1, keepdims=True) + EPS)
    return centred * r, r


def norm_back(v, e, gain):
    n, r = norm_parts(v)
    eg = e * gain
    grad = r * (
        eg
        - jnp.mean(eg, axis=1, keepdims=True)
        - n * jnp.mean(eg * n, axis=1, keepdims=True)
    )
    return grad, n


def col_sum(v):
    return jnp.sum(v, axis=0, keepdims=True)


def head_part(v, h):
    lane = lax.broadcasted_iota(jnp.int32, v.shape, 1)
    return jnp.where((lane >= HD * h) & (lane < HD * h + HD), v, jnp.zeros_like(v))


class Place:
    def __init__(self):
        dp = lax.axis_index("dp")
        self.t = t = lax.axis_index("tensor")
        self.z = dp // 8
        self.yl = (dp // 4) % 2
        self.x = dp % 4
        self.c = t % 2
        self.yh = t // 2
        self.t_sib = t + 1 - 2 * self.c
        self.t_part = (t + 2) % 4
        self.t_far = (self.t_sib + 2) % 4
        self.sib = (dp, self.t_sib)
        self.part = (dp, self.t_part)
        self.ypeer = (dp + 4 - 8 * self.yl, t)
        self.dp = dp

    def xpeer(self, j):
        return (self.dp - self.x + (self.x + j) % 4, self.t)

    def zpeer(self, j):
        return (((self.z + j) % 4) * 8 + self.dp % 8, self.t)

    def peers(self):
        return (
            [self.sib, self.part, self.ypeer]
            + [self.xpeer(j) for j in (1, 2, 3)]
            + [self.zpeer(j) for j in (1, 2, 3)]
        )


def remote(src, dst, send, recv, device):
    return pltpu.make_async_remote_copy(
        src_ref=src,
        dst_ref=dst,
        send_sem=send,
        recv_sem=recv,
        device_id=device,
        device_id_type=MESH,
    )


class Reduction:
    def __init__(self, at, stg, r1, r2, ry, send, recv, free):
        self.at, self.stg, self.r1, self.r2, self.ry = at, stg, r1, r2, ry
        self.send, self.recv, self.free = send, recv, free
        self.big = stg.shape[0] // 4
        self.small = stg.shape[0] // 16

    def axes(self, h):
        at = self.at
        if h == 0:
            return at.x, at.z, at.xpeer, at.zpeer
        return at.z, at.x, at.zpeer, at.xpeer

    def block(self, h, first):
        rows = pl.ds(pl.multiple_of(first * self.big, self.big), self.big)
        return self.stg.at[rows, pl.ds(h * 384, 384)]

    def part(self, h, first, second):
        start = pl.multiple_of(first * self.big + second * self.small, self.small)
        return self.stg.at[pl.ds(start, self.small), pl.ds(h * 384, 384)]

    def copy(self, h, step, src, dst, device):
        return remote(src, dst, self.send.at[h, step], self.recv.at[h, step], device)

    def out1(self, h, j):
        first, _, peer, _ = self.axes(h)
        return self.copy(h, j - 1, self.block(h, (first + j) % 4), self.r1.at[h, j - 1], peer(j))

    def out2(self, h, j):
        first, second, _, peer = self.axes(h)
        return self.copy(
            h, 2 + j, self.part(h, first, (second + j) % 4), self.r2.at[h, j - 1], peer(j)
        )

    def outy(self, h):
        first, second, _, _ = self.axes(h)
        return self.copy(h, 6, self.part(h, first, second), self.ry.at[h], self.at.ypeer)

    def back2(self, h, j, arriving=False):
        first, second, _, peer = self.axes(h)
        own = self.part(h, first, (second + 4 - j) % 4 if arriving else second)
        return self.copy(h, 6 + j, own, own, peer(j))

    def back1(self, h, j, arriving=False):
        first, _, peer, _ = self.axes(h)
        own = self.block(h, (first + 4 - j) % 4 if arriving else first)
        return self.copy(h, 9 + j, own, own, peer(j))

    def give_back(self, h, stage):
        peer = self.axes(h)[2 + stage]
        for j in (1, 2, 3):
            (self.out1 if stage == 0 else self.out2)(h, j).wait_send()
        for j in (1, 2, 3):
            pl.semaphore_signal(
                self.free.at[h, stage], inc=1, device_id=peer(j), device_id_type=MESH
            )

    def start(self):
        for h in (0, 1):
            for j in (1, 2, 3):
                self.out1(h, j).start()

    def second(self):
        for h in (0, 1):
            for j in (1, 2, 3):
                self.out1(h, j).wait_recv()
            own = self.block(h, self.axes(h)[0])
            total = own[...].astype(F32)
            for j in (0, 1, 2):
                total = total + self.r1[h, j].astype(F32)
            own[...] = total.astype(BF)
            for j in (1, 2, 3):
                self.out2(h, j).start()
            self.give_back(h, 0)

    def third(self):
        for h in (0, 1):
            for j in (1, 2, 3):
                self.out2(h, j).wait_recv()
            first, second, _, _ = self.axes(h)
            own = self.part(h, first, second)
            total = own[...].astype(F32)
            for j in (0, 1, 2):
                total = total + self.r2[h, j].astype(F32)
            own[...] = total.astype(BF)
            self.outy(h).start()
            self.give_back(h, 1)

    def fourth(self):
        for h in (0, 1):
            self.outy(h).wait()
            first, second, _, _ = self.axes(h)
            own = self.part(h, first, second)
            own[...] = (own[...].astype(F32) + self.ry[h].astype(F32)).astype(BF)
            pl.semaphore_wait(self.free.at[h, 1], 3)
            for j in (1, 2, 3):
                self.back2(h, j).start()

    def fifth(self):
        for h in (0, 1):
            for j in (1, 2, 3):
                self.back2(h, j, True).wait_recv()
            pl.semaphore_wait(self.free.at[h, 0], 3)
            for j in (1, 2, 3):
                self.back1(h, j).start()

    def finish(self):
        for h in (0, 1):
            for j in (1, 2, 3):
                self.back1(h, j, True).wait_recv()

    def drain(self):
        for h in (0, 1):
            for j in (1, 2, 3):
                self.back2(h, j).wait_send()
                self.back1(h, j).wait_send()


def kernel(
    comm,
    x_hbm,
    cot_hbm,
    wqkv_hbm,
    wout_hbm,
    wup_hbm,
    wdown_hbm,
    flags_ref,
    mask_ref,
    bqv_ref,
    gain1_ref,
    shift1_ref,
    bout_ref,
    gain2_ref,
    shift2_ref,
    bup_ref,
    bdown_ref,
    res,
    gin,
    stg_u,
    stg_d,
    stg_q,
    small_ref,
    x_ref,
    u_ref,
    wqkv,
    wof,
    wup,
    wdown,
    fwup,
    fwdown,
    bias,
    fbias,
    n1,
    q8,
    keys,
    vals,
    att,
    lse,
    mid,
    n2,
    nt2,
    actt,
    own_a,
    own_b,
    s1,
    r1,
    sd,
    rd,
    s2,
    r2,
    mlow,
    gp,
    sc,
    pr,
    ds,
    red1,
    red2,
    redy,
    weight,
    sm,
    smp,
    smc,
    smx,
    smz,
    smy,
    in_sem,
    a_send,
    a_recv,
    w_send,
    w_recv,
    t_send,
    t_recv,
    d_send,
    d_recv,
    d_free,
    m_send,
    m_recv,
):
    at = Place()
    c, yh, t = (at.c, at.yh, at.t) if comm else (0, 0, 0)
    ghid = gin
    gpt = nt2.at[0:576]

    def lanes(s, half=None):
        if half is None:
            return pl.ds(pl.multiple_of(s * LEN, LEN), LEN)
        return pl.ds(pl.multiple_of(s * LEN + half * HALF, HALF), HALF)

    def core_rows(core):
        return pl.ds(pl.multiple_of(core * QUART, QUART), QUART)

    def flat(v):
        return v.reshape(-1, v.shape[-1])

    def wout_rows(t, start, count):
        return wof.at[pl.ds(pl.multiple_of(t * 192 + start, 48), count)]

    def wout_block(t):
        return wout_rows(t, 0, 192)

    def att_block(s):
        return lambda t: att.at[s, pl.ds(pl.multiple_of(t * 192, 192), 192)]

    def row_block(ref, s):
        return lambda t: ref.at[s, t // 2, t % 2]

    def load(i, src, dst):
        return pltpu.make_async_copy(src, dst, in_sem.at[i])

    def load_x(s):
        return load(s, x_hbm.at[s], x_ref.at[s])

    load_wqkv = load(3, wqkv_hbm, wqkv)
    load_wout = load(4, wout_hbm, wout_block(t))
    load_cot = load(5, cot_hbm, u_ref)
    load_up = load(6, wup_hbm, wup)
    load_down = load(7, wdown_hbm, wdown)
    load_wout.start()
    load_up.start()
    load_down.start()
    load_x(0).start()
    load_wqkv.start()
    load_x(1).start()
    load_x(2).start()
    load_cot.start()

    sm[...] = jnp.zeros_like(sm)
    bias[...] = jnp.broadcast_to(bup_ref[...].reshape(1, D), (8, D))
    weight[...] = jnp.maximum(flags_ref[...], mask_ref[...]).astype(F32).reshape(2 * SEQS, HALF)
    if comm:
        barrier = pltpu.get_barrier_semaphore()
        peers = at.peers()
        for peer in peers:
            pl.semaphore_signal(barrier, inc=1, device_id=peer, device_id_type=MESH)
        pl.semaphore_wait(barrier, len(peers))

    def fetch_part(i, count):
        first, second = (at.x, at.z) if i == 0 else (at.z, at.x)
        start = (second * 4 + (first if count == 1 else 0)) * 48
        return pl.ds(pl.multiple_of(start, 48), 48 * count)

    def fetch_copy(i, step, src, dst, device):
        return remote(src, dst, w_send.at[i, step], w_recv.at[i, step], device)

    def fetch_y(i):
        if i == 2:
            ref = wout_rows(t, at.x * 48, 48)
            return fetch_copy(i, 0, ref, ref, at.part)
        src, dst = ((wup, fwup), (wdown, fwdown))[i]
        some = fetch_part(i, 1)
        return fetch_copy(i, 0, src.at[some], dst.at[some], at.part)

    def fetch_a(i, j):
        peer = at.zpeer if i == 1 else at.xpeer
        ref = wout_rows(at.t_part, at.x * 48, 48) if i == 2 else (fwup, fwdown)[i].at[fetch_part(i, 1)]
        return fetch_copy(i, j, ref, ref, peer(j))

    def fetch_b(i, j):
        peer = at.xpeer if i == 1 else at.zpeer
        ref = (fwup, fwdown)[i].at[fetch_part(i, 4)]
        return fetch_copy(i, 3 + j, ref, ref, peer(j))

    fetch_bias = remote(bias, fbias, w_send.at[2, 4], w_recv.at[2, 4], at.part)

    def fetch_first():
        if comm:
            for i in (2, 0, 1):
                fetch_y(i).start()
            fetch_bias.start()

    def fetch_second():
        if comm:
            for i in (2, 0, 1):
                fetch_y(i).wait_recv()
                for j in (1, 2, 3):
                    fetch_a(i, j).start()

    def fetch_third():
        if comm:
            for i in (2, 0, 1):
                for j in (1, 2, 3):
                    fetch_a(i, j).wait_recv()
                if i < 2:
                    for j in (1, 2, 3):
                        fetch_b(i, j).start()

    def fetch_wait():
        if comm:
            fetch_bias.wait_recv()
            for i in (0, 1):
                for j in (1, 2, 3):
                    fetch_b(i, j).wait_recv()

    def fetch_drain():
        if comm:
            fetch_bias.wait_send()
            for i in (2, 0, 1):
                fetch_y(i).wait_send()
                for j in (1, 2, 3):
                    fetch_a(i, j).wait_send()
                    if i < 2:
                        fetch_b(i, j).wait_send()

    def gather_copy(i, block, kind, t, device):
        ref = block(t)
        return remote(ref, ref, a_send.at[i, kind], a_recv.at[i, kind], device)

    def gather_start(i, block):
        if comm:
            if not isinstance(i, int) or i != 3:
                gather_copy(i, block, 1, at.t, at.part).start()
            gather_copy(i, block, 0, at.t, at.sib).start()

    def gather_forward(i, block):
        if comm:
            if not isinstance(i, int) or i != 3:
                gather_copy(i, block, 1, at.t_part, at.part).wait_recv()
            gather_copy(i, block, 2, at.t_part, at.sib).start()

    def gather_wait(i, block):
        if comm:
            gather_copy(i, block, 0, at.t_sib, at.sib).wait_recv()
            gather_copy(i, block, 2, at.t_far, at.sib).wait_recv()

    def gather_drain(i, block):
        if comm:
            gather_copy(i, block, 0, at.t, at.sib).wait_send()
            if i != 3:
                gather_copy(i, block, 1, at.t, at.part).wait_send()
            gather_copy(i, block, 2, at.t_part, at.sib).wait_send()

    def core_copy(k, s):
        return remote(s1.at[k, s], r1.at[k, s], t_send.at[k, s], t_recv.at[k, s], at.sib)

    def core_sum(k, s, own):
        if comm:
            core_copy(k, s).wait()
        return own[s, core_rows(c), :] + r1[k, s].astype(F32)

    def chip_copy(s):
        return remote(sd.at[s], rd.at[s], t_send.at[2, s], t_recv.at[2, s], at.sib)

    def group_copy(s):
        return remote(s2.at[s], r2.at[s], t_send.at[3, s], t_recv.at[3, s], at.part)

    def share_copy(s, core):
        ref = gin.at[s, :, core]
        return remote(ref, ref, t_send.at[4, s], t_recv.at[4, s], at.sib)

    def chip_sum(s):
        if comm:
            chip_copy(s).wait()
        total = own_a[s] + flat(rd[s]).astype(F32)
        s2[s] = total.astype(BF).reshape(2, QUART, D)
        if comm:
            group_copy(s).start()

    gain1, shift1, gain2, shift2, b_out, b_down = (
        ref[...].reshape(1, D)
        for ref in (gain1_ref, shift1_ref, gain2_ref, shift2_ref, bout_ref, bdown_ref)
    )

    def add_small(row, value):
        sm[row : row + 1, :] += value

    def attend(s):
        load_x(s).wait()
        n, _r = norm_parts(flat(x_ref[s]).astype(F32))
        normed = (n * gain1 + shift1).astype(BF)
        n1[s] = normed
        q = (dot(normed, wqkv[0], NT) + bqv_ref[0:1, :]).astype(BF) * SCALE
        q8[s] = q
        k = dot(normed, wqkv[1], NT).astype(BF)
        keys[s] = k
        v = (dot(normed, wqkv[2], NT) + bqv_ref[1:2, :]).astype(BF)
        vals[s] = v
        vt = v.T
        block = att_block(s)(t)
        for h in range(3):
            sc[...] = dot(head_part(k, h), q, NT)
            for part in range(4):
                cols = slice(part * 128, part * 128 + 128)
                scores = sc[:, cols]
                top = jnp.max(scores, axis=0, keepdims=True)
                e = jnp.exp(scores - top)
                total = col_sum(e)
                lse[3 * s + h, :, cols] = top + jnp.log(total)
                pr[:, cols] = (e * (1.0 / total)).astype(BF)
            mixed = dot(vt[HD * h : HD * h + HD], pr[...], NN)
            block[HD * h : HD * h + HD, :] = mixed.astype(BF)
        gather_start(s, att_block(s))

    def weigh(i, _):
        same = lax.broadcasted_iota(jnp.int32, (HALF, HALF), 0) == lax.broadcasted_iota(
            jnp.int32, (HALF, HALF), 1
        )
        diagonal = jnp.where(same, weight[pl.ds(i, 1), :], 0.0).astype(BF)
        rows = dot(diagonal, flat(u_ref[i // 2, i % 2]), NN).astype(BF)
        u_ref[i // 2, i % 2] = rows.reshape(2, QUART, D)
        return 0

    def hidden_units(normed, up, w_up, b_up, w_down):
        v = dot(normed, w_up[...], NN) + b_up
        back = dot(up, w_down[...], NT)
        square = v * v
        th = jnp.tanh(GELU_A * (v + GELU_B * square * v))
        cdf = 0.5 * (1.0 + th)
        slope = cdf + (0.5 * GELU_A) * v * (1.0 - th * th) * (1.0 + (3.0 * GELU_B) * square)
        return (v * cdf).astype(BF), back * slope

    def feed(s, _):
        gather_wait(s, att_block(s))
        for own in (False, True):
            half = yh if own else 1 - yh
            some = lanes(s, half)
            cols = pl.ds(pl.multiple_of(half * HALF, HALF), HALF)
            middle = flat(x_ref[s, half]).astype(F32) + dot(att[s, :, cols], wof[...], TN) + b_out
            n, _r = norm_parts(middle)
            normed = (n * gain2 + shift2).astype(BF)
            nt2[:, some] = normed.T
            act, grad = hidden_units(normed, flat(u_ref[s, half]), wup, bias[0:1, :], wdown)
            add_small(BUP, col_sum(grad))
            grad = grad.astype(BF)
            actt[:, some] = act.T
            ghid[s, half] = grad.reshape(2, QUART, D)
            if own:
                mid[s] = middle
                n2[s] = normed
                own_a[s] = dot(grad, wup[...], NT)
                own_b[s] = dot(act, wdown[...], NN)
            else:

                @pl.when(s < SEQS - 1)
                def _():
                    gather_forward(s + 1, att_block(s + 1))

        return 0

    def feed_more(s):
        act, grad = hidden_units(n2[s], flat(u_ref[s, yh]), fwup, fbias[0:1, :], fwdown)
        own_a[s] += dot(grad.astype(BF), fwup[...], NT)
        own_b[s] += dot(act, fwdown[...], NN)
        for k, ref in enumerate((own_a, own_b)):
            s1[k, s] = ref[s, core_rows(1 - c), :].astype(BF)
            if comm:
                core_copy(k, s).start()

    def middle_back(s):
        e = core_sum(0, s, own_a)
        grad, n = norm_back(mid[s, core_rows(c), :], e, gain2)
        add_small(GAIN2, col_sum(e * n))
        add_small(SHIFT2, col_sum(e))
        up = u_ref[s, yh, c].astype(F32)
        grad = up + grad
        add_small(BOUT, col_sum(grad))
        add_small(BDOWN, col_sum(up))
        mlow[s, yh, c] = grad.astype(BF)
        gather_start(4 + s, row_block(mlow, s))

    def output_rows(s):
        total = mid[s, core_rows(c), :] + core_sum(1, s, own_b) + b_down
        res[s, yh, c] = total.astype(BF)
        gather_start(7 + s, row_block(res, s))

    d_up, d_down, d_qkv = (
        Reduction(
            at, ref, red1.at[i], red2.at[i], redy.at[i], d_send.at[i], d_recv.at[i], d_free.at[i]
        )
        for i, ref in enumerate((stg_u, stg_d, stg_q))
    )

    def reduce_step(name, which):
        if comm:
            getattr(which, name)()

    def stage(stg, start, count, value):
        stg[pl.ds(start, count), :] = value.astype(BF)

    def up_grads(i, _):
        start = pl.multiple_of(i * HALF, HALF)
        some = pl.ds(start, HALF)
        stage(stg_u, start, HALF, dot(nt2[some, :], flat(ghid[...]), NN))
        return 0

    def down_grads(i, _):
        start = pl.multiple_of(i * HALF, HALF)
        some = pl.ds(start, HALF)
        stage(stg_d, start, HALF, dot(actt[some, :], flat(u_ref[...]), NN))
        return 0

    def qkv_grads(i, _):
        start = pl.multiple_of(i * 192, 192)
        stage(stg_q, start, 192, dot(gpt[pl.ds(start, 192), :], flat(n1[...]), NN))
        return 0

    def out_grads():
        total = jnp.zeros((192, D), F32)
        for s in range(SEQS):
            total += dot(att_block(s)(t)[...], flat(mlow[s]), NN)
        stage(stg_q, 576, 192, total)

    def attend_back(s, between):
        gather_wait(4 + s, row_block(mlow, s))
        some_lanes = lanes(s)
        mixed = dot(flat(mlow[s]), wout_block(t)[...], NT).astype(BF)
        q, k, v = q8[s], keys[s], vals[s]
        kt = k.T
        grad_k = jnp.zeros((LEN, 192), F32)
        grad_v = jnp.zeros((LEN, 192), F32)
        for h in range(3):
            sc[...] = dot(head_part(k, h), q, NT)
            back = dot(head_part(v, h), mixed, NT)
            some = slice(HD * h, HD * h + HD)
            for part in range(4):
                cols = slice(part * 128, part * 128 + 128)
                p = jnp.exp(sc[:, cols] - lse[3 * s + h, :, cols])
                pr[:, cols] = p.astype(BF)
                gp_part = back[:, cols]
                total = col_sum(gp_part * p)
                ds[:, cols] = (p * (gp_part - total)).astype(BF)
            grad_v += dot(pr[...], head_part(mixed, h), NN)
            grad_k += dot(ds[...], head_part(q, h), NN)
            gpt[some, some_lanes] = (dot(kt[some], ds[...], NN) * SCALE).astype(BF)
        grad_q = gpt[0:192, some_lanes].T
        grad_k = grad_k.astype(BF)
        grad_v = grad_v.astype(BF)
        gpt[192:384, some_lanes] = grad_k.T
        gpt[384:576, some_lanes] = grad_v.T
        for i, grad in enumerate((grad_q, grad_k, grad_v)):
            gp[i] = grad.reshape(2, 2, QUART, 192)
        sm[BQV : BQV + 1, 0:192] += col_sum(grad_q.astype(F32))
        sm[BQV : BQV + 1, 256:448] += col_sum(grad_v.astype(F32))
        between()
        for own in (False, True):
            core = c if own else 1 - c
            total = dot(flat(gp[0, :, core]), wqkv[0], NN)
            total += dot(flat(gp[1, :, core]), wqkv[1], NN)
            total += dot(flat(gp[2, :, core]), wqkv[2], NN)
            if own:
                own_a[s] = total
            else:
                sd[s] = total.astype(BF).reshape(2, QUART, D)
                if comm:
                    chip_copy(s).start()

    def input_back(s):
        if comm:
            group_copy(s).wait()
        e = flat(s2[s]).astype(F32) + flat(r2[s]).astype(F32)
        grad, n = norm_back(flat(x_ref[s, :, c]).astype(F32), e, gain1)
        add_small(GAIN1, col_sum(e * n))
        add_small(SHIFT1, col_sum(e))
        total = flat(mlow[s, :, c]).astype(F32) + grad
        gin[s, :, c] = total.astype(BF).reshape(2, QUART, D)
        if comm:
            share_copy(s, c).start()

    def finish_out(s):
        gather_wait(7 + s, row_block(res, s))

    def finish_gin(s):
        if comm:
            share_copy(s, 1 - c).wait_recv()

    def small_copy(i, slots, slot, device):
        ref = slots.at[slot]
        return remote(ref, ref, m_send.at[i], m_recv.at[i], device)

    def small_row():
        return lax.broadcasted_iota(jnp.int32, (8, D), 0)

    def small_part():
        smp[yh] = sm[...]
        if comm:
            small_copy(8, smp, yh, at.part).start()

    def small_chip():
        small_copy(8, smp, 1 - yh, at.part).wait_recv()
        row = small_row()
        smc[c] = jnp.where((row >= GAIN2) & (row < BUP), smp[0] + smp[1], sm[...])
        small_copy(0, smc, c, at.sib).start()

    def small_x():
        small_copy(0, smc, 1 - c, at.sib).wait_recv()
        smx[at.x] = jnp.where(small_row() < BUP, smc[0] + smc[1], smc[c])
        for j in (1, 2, 3):
            small_copy(j, smx, at.x, at.xpeer(j)).start()

    def small_z():
        for j in (1, 2, 3):
            small_copy(j, smx, (at.x + 4 - j) % 4, at.xpeer(j)).wait_recv()
        smz[at.z] = (smx[0] + smx[1]) + (smx[2] + smx[3])
        for j in (1, 2, 3):
            small_copy(3 + j, smz, at.z, at.zpeer(j)).start()

    def small_y():
        for j in (1, 2, 3):
            small_copy(3 + j, smz, (at.z + 4 - j) % 4, at.zpeer(j)).wait_recv()
        smy[at.yl] = (smz[0] + smz[1]) + (smz[2] + smz[3])
        small_copy(7, smy, at.yl, at.ypeer).start()

    def small_end():
        small_copy(7, smy, 1 - at.yl, at.ypeer).wait_recv()
        small_ref[...] = smy[0] + smy[1]

    def small_drain():
        small_copy(8, smp, yh, at.part).wait_send()
        small_copy(0, smc, c, at.sib).wait_send()
        for j in (1, 2, 3):
            small_copy(j, smx, at.x, at.xpeer(j)).wait_send()
            small_copy(3 + j, smz, at.z, at.zpeer(j)).wait_send()
        small_copy(7, smy, at.yl, at.ypeer).wait_send()

    load_up.wait()
    load_down.wait()
    load_wout.wait()
    fetch_first()
    gather_start(3, wout_block)
    load_wqkv.wait()

    def attend_all(s, _):
        attend(s)

        @pl.when(s == 1)
        def _():
            fetch_second()

        return 0

    lax.fori_loop(0, SEQS, attend_all, 0)
    load_cot.wait()
    lax.fori_loop(0, 2 * SEQS, weigh, 0)
    gather_forward(0, att_block(0))
    fetch_third()
    gather_forward(3, wout_block)
    gather_wait(3, wout_block)
    lax.fori_loop(0, SEQS, feed, 0)
    lax.fori_loop(0, 3, up_grads, 0)
    reduce_step("start", d_up)
    fetch_wait()
    feed_more(0)
    feed_more(1)
    middle_back(0)
    feed_more(2)
    middle_back(1)
    lax.fori_loop(0, 3, down_grads, 0)
    middle_back(2)
    small_part()
    reduce_step("second", d_up)
    reduce_step("start", d_down)
    gather_forward(4, row_block(mlow, 0))

    def attend_back_all(s, _):
        def between():
            @pl.when(s < SEQS - 1)
            def _():
                gather_forward(5 + s, row_block(mlow, s + 1))

            @pl.when(s == 0)
            def _():
                reduce_step("third", d_up)
                output_rows(0)

            @pl.when(s == 1)
            def _():
                reduce_step("fourth", d_up)
                reduce_step("second", d_down)

            @pl.when(s == 2)
            def _():
                reduce_step("fifth", d_up)
                reduce_step("third", d_down)

            @pl.when(s > 0)
            def _():
                chip_sum(s - 1)

        attend_back(s, between)
        return 0

    lax.fori_loop(0, SEQS, attend_back_all, 0)
    lax.fori_loop(0, 3, qkv_grads, 0)
    out_grads()
    reduce_step("start", d_qkv)
    chip_sum(2)
    input_back(0)
    gather_forward(7, row_block(res, 0))
    reduce_step("fourth", d_down)
    finish_gin(0)
    finish_out(0)
    reduce_step("second", d_qkv)
    reduce_step("fifth", d_down)
    input_back(1)
    finish_gin(1)
    reduce_step("third", d_qkv)
    output_rows(1)
    output_rows(2)
    input_back(2)
    if comm:
        small_chip()
    finish_gin(2)
    if comm:
        small_x()
    reduce_step("fourth", d_qkv)
    if comm:
        small_z()
    reduce_step("fifth", d_qkv)
    if comm:
        small_y()
    gather_forward(8, row_block(res, 1))
    reduce_step("finish", d_up)
    reduce_step("finish", d_down)
    gather_forward(9, row_block(res, 2))
    finish_out(1)
    if comm:
        small_end()
    else:
        small_ref[...] = sm[...]
    finish_out(2)
    reduce_step("finish", d_qkv)

    if comm:
        fetch_drain()
        gather_drain(3, wout_block)
        for s in range(SEQS):
            gather_drain(s, att_block(s))
            gather_drain(4 + s, row_block(mlow, s))
            gather_drain(7 + s, row_block(res, s))
            share_copy(s, c).wait_send()
        for which in (d_up, d_down, d_qkv):
            which.drain()
        small_drain()


def layer(comm, x, cot, *rest):
    rows = (SEQS, 2, 2, QUART, D)
    half = (SEQS, HALF, D)
    pair = (SEQS, 2, QUART, D)
    dma = pltpu.SemaphoreType.DMA
    scratch = [
        pltpu.VMEM(rows, BF),
        pltpu.VMEM(rows, BF),
        pltpu.VMEM((3, 192, D), BF),
        pltpu.VMEM((D, D), BF),
        pltpu.VMEM((D, D), BF),
        pltpu.VMEM((D, D), BF),
        pltpu.VMEM((D, D), BF),
        pltpu.VMEM((D, D), BF),
        pltpu.VMEM((8, D), F32),
        pltpu.VMEM((8, D), F32),
        pltpu.VMEM((SEQS, LEN, D), BF),
        pltpu.VMEM((SEQS, LEN, 192), BF),
        pltpu.VMEM((SEQS, LEN, 192), BF),
        pltpu.VMEM((SEQS, LEN, 192), BF),
        pltpu.VMEM((SEQS, D, LEN), BF),
        pltpu.VMEM((3 * SEQS, 1, LEN), F32),
        pltpu.VMEM(half, F32),
        pltpu.VMEM(half, BF),
        pltpu.VMEM((D, ROWS), BF),
        pltpu.VMEM((D, ROWS), BF),
        pltpu.VMEM(half, F32),
        pltpu.VMEM(half, F32),
        pltpu.VMEM((2, SEQS, QUART, D), BF),
        pltpu.VMEM((2, SEQS, QUART, D), BF),
        pltpu.VMEM(pair, BF),
        pltpu.VMEM(pair, BF),
        pltpu.VMEM(pair, BF),
        pltpu.VMEM(pair, BF),
        pltpu.VMEM(rows, BF),
        pltpu.VMEM((3, 2, 2, QUART, 192), BF),
        pltpu.VMEM((LEN, LEN), F32),
        pltpu.VMEM((LEN, LEN), BF),
        pltpu.VMEM((LEN, LEN), BF),
        pltpu.VMEM((3, 2, 3, 192, 384), BF),
        pltpu.VMEM((3, 2, 3, 48, 384), BF),
        pltpu.VMEM((3, 2, 48, 384), BF),
        pltpu.VMEM((2 * SEQS, HALF), F32),
        pltpu.VMEM((8, D), F32),
        pltpu.VMEM((2, 8, D), F32),
        pltpu.VMEM((2, 8, D), F32),
        pltpu.VMEM((4, 8, D), F32),
        pltpu.VMEM((4, 8, D), F32),
        pltpu.VMEM((2, 8, D), F32),
        dma((8,)),
        dma((10, 3)),
        dma((10, 3)),
        dma((3, 7)),
        dma((3, 7)),
        dma((5, SEQS)),
        dma((5, SEQS)),
        dma((3, 2, 13)),
        dma((3, 2, 13)),
        pltpu.SemaphoreType.REGULAR((3, 2, 2)),
        dma((9,)),
        dma((9,)),
    ]
    anywhere = pl.BlockSpec(memory_space=pl.ANY)
    vmem = pl.BlockSpec(memory_space=pltpu.VMEM)
    return pl.pallas_call(
        functools.partial(kernel, comm),
        out_shape=(
            pltpu.VMEM(rows, BF),
            pltpu.VMEM(rows, BF),
            pltpu.VMEM((D, D), BF),
            pltpu.VMEM((D, D), BF),
            pltpu.VMEM((D, D), BF),
            pltpu.VMEM((8, D), F32),
        ),
        in_specs=[anywhere] * 6 + [vmem] * 10,
        out_specs=(vmem,) * 6,
        scratch_shapes=scratch,
        compiler_params=pltpu.CompilerParams(
            collective_id=0 if comm else None,
            has_side_effects=True,
            vmem_limit_bytes=54 * 2**20,
        ),
        cost_estimate=pl.CostEstimate(
            flops=20 * 10**9, bytes_accessed=20 * 10**6, transcendentals=10**7
        ),
        name="layer",
    )(x.reshape(rows), cot.reshape(rows), *rest)


def shards(
    layer_input,
    flags,
    loss_mask,
    cotangent,
    gain_one,
    shift_one,
    w_qkv,
    b_qv,
    w_out,
    b_out,
    gain_two,
    shift_two,
    w_up,
    b_up,
    w_down,
    b_down,
    comm=True,
):
    out, gin, g_up, g_down, g_qkv, small = layer(
        comm,
        layer_input,
        cotangent,
        w_qkv.transpose(0, 2, 1),
        w_out,
        w_up,
        w_down,
        flags,
        loss_mask,
        b_qv,
        gain_one,
        shift_one,
        b_out,
        gain_two,
        shift_two,
        b_up,
        b_down,
    )
    return (
        out.reshape(ROWS, D),
        gin.reshape(ROWS, D),
        small[GAIN1],
        small[SHIFT1],
        g_qkv[:576].reshape(3, 192, D).transpose(0, 2, 1).astype(F32),
        jnp.stack([small[BQV, 0:192], small[BQV, 256:448]]),
        g_qkv[576:].astype(F32),
        small[BOUT],
        small[GAIN2],
        small[SHIFT2],
        g_up.astype(F32),
        small[BUP],
        g_down.astype(F32),
        small[BDOWN],
    )


def solution(mesh):
    in_specs = (
        P("dp", None),
        P("dp"),
        P("dp"),
        P("dp", None),
        P(),
        P(),
        P(None, None, "tensor"),
        P(None, "tensor"),
        P("tensor", None),
        P(),
        P(),
        P(),
        P(None, "tensor"),
        P("tensor"),
        P("tensor", None),
        P(),
    )
    out_specs = (
        P("dp", None),
        P("dp", None),
        P(),
        P(),
        P(None, None, "tensor"),
        P(None, "tensor"),
        P("tensor", None),
        P(),
        P(),
        P(),
        P(None, "tensor"),
        P("tensor"),
        P("tensor", None),
        P(),
    )
    return jax.shard_map(shards, mesh=mesh, in_specs=in_specs, out_specs=out_specs, check_vma=False)
```

time: 152 us -> 121 us (0.80)
  Pallas kernels: 131 us -> 110 us
  local copies, waits for them, and re-layouts: 17 us -> 3.53 us
  other arithmetic: 2.65 us -> 5.94 us
    pallas_call x1, Pallas kernels: 131 us -> 110 us  [layer(): pl.pallas_call(functools.partial(kernel, comm), out_shape=(pltpu.VMEM(row...]
    another operation x7 -> x0, local copies, waits for them, and re-layouts: 4.77 us -> none  [shards(): vecs = jnp.stack([gain_one, shift_one, gain_two, shift_two, b_out, b_down])]
    convert_element_type x3 -> x4, other arithmetic: 1.21 us -> 5.36 us  [the longest x1 1.58 us: shards(): g_up.astype(F32)]
    slice x2 -> x1, local copies, waits for them, and re-layouts: 3.81 us -> 0.06 us  [shards(): g_qkv[:576].reshape(3, 192, D).transpose(0, 2, 1).astype(F32)]
    reshape x2 -> x0, local copies, waits for them, and re-layouts: 1.87 us -> none  [the longest x1 1.27 us: shards(): b_up.reshape(1, D)]
    squeeze x2 -> x0, local copies, waits for them, and re-layouts: 1.6 us -> none  [the longest x1 1.36 us: shards(): g1 = jnp.concatenate([g1[0], g1[1]], axis=1).astype(F32)]
    unnamed x10 -> x2, local copies, waits for them, and re-layouts: 4.32 us -> 2.81 us
where the time goes in v2:
time: 121 us; the launch traced here: 120 us
  Pallas kernels  110 us (91%)
  other arithmetic  5.94 us (5%)
  local copies, waits for them, and re-layouts  3.53 us (3%)
    pallas_call x1, Pallas kernels, layer(): pl.pallas_call(functools.partial(kernel, comm), out_shape=(pltpu.VMEM(row...  110 us
    unnamed x2, local copies, waits for them, and re-layouts  2.81 us

profile of v2, /device:TPU:0, one launch (start us, length us, event | category | flops | bytes accessed | tf_op | source)
XLA Modules:
  0.0 120.3 jit_solution(5667221960105554494)
XLA Ops:
  0.7 110.1 %layer.1 = (bf16[3,2,2,128,768]{4,3,2,1,0:T(8,128)(2,1)S(1)}, bf16[3,2,2,128,768]{4,3,2,1,0:T(8,128)(2,1)S(1)}, bf16[768,768]{1,0:T(8,128)(2,1)S(1)}, bf16[768,7...) custom-call(bf16[3,2,2,128,768]{4,3,2,1,0:T(8,128)(2,1)} %bitcast.12, ...), custom_call_target="tpu_custom_call" | custom-call | flops 20000000000 | bytes 20000000 | tf_op jit(solution)/shard_map/layer/pallas_call | solution.py:922
  110.8 1.4 %copy.32 = bf16[1536,768]{1,0:T(8,128)(2,1)} copy(bf16[1536,768]{1,0:T(8,128)(2,1)S(1)} %bitcast.10) | data formatting | bytes 4718592
  112.2 1.4 %copy.33 = bf16[1536,768]{1,0:T(8,128)(2,1)} copy(bf16[1536,768]{1,0:T(8,128)(2,1)S(1)} %bitcast.9) | data formatting | bytes 4718592
  113.6 0.6 pad_maximum_fusion
  114.2 0.7 slice_reduce_fusion
  114.8 0.9 slice_convert_fusion
  115.7 0.1 slice.35
  115.8 1.4 %convert_bitcast_fusion = f32[3,768,192]{1,2,0:T(8,128)} fusion(bf16[3,192,768]{2,1,0:T(8,128)(2,1)S(1)} %bitcast.11), kind=kLoop, calls=%fused_computation | loop fusion | flops 442368 | bytes 2654208 | tf_op jit(solution)/shard_map/convert_element_type | solution.py:990
  117.1 1.6 %convert_element_type.22 = f32[768,768]{1,0:T(8,128)} convert(bf16[768,768]{1,0:T(8,128)(2,1)S(1)} %get-tuple-element.24) | non-fusion elementwise | flops 589824 | bytes 3538944 | tf_op jit(solution)/shard_map/convert_element_type | solution.py:996
  118.7 1.6 %convert_element_type.23 = f32[768,768]{1,0:T(8,128)} convert(bf16[768,768]{1,0:T(8,128)(2,1)S(1)} %get-tuple-element.25) | non-fusion elementwise | flops 589824 | bytes 3538944 | tf_op jit(solution)/shard_map/convert_element_type | solution.py:998
  (1 shorter events, 0.0 us)

commit v3 on v2

v3 whole, which is shorter than its diff:
```python
import functools

import jax
import jax.numpy as jnp
from jax import lax
from jax.experimental import pallas as pl
from jax.experimental.pallas import tpu as pltpu
from jax.sharding import PartitionSpec as P

MESH = pl.DeviceIdType.MESH
BF = jnp.bfloat16
F32 = jnp.float32
D = 768
HD = 64
LEN = 512
HALF = 256
QUART = 128
SEQS = 3
ROWS = SEQS * LEN
EPS = 1e-05
SCALE = HD**-0.5
GELU_A = 0.7978845608028654
GELU_B = 0.044715

NN = (((1,), (0,)), ((), ()))
NT = (((1,), (1,)), ((), ()))
TN = (((0,), (0,)), ((), ()))

GAIN1, SHIFT1, GAIN2, SHIFT2, BOUT, BDOWN, BUP, BQV = range(8)


def dot(a, b, dims):
    return lax.dot_general(a, b, dims, preferred_element_type=F32)


def norm_parts(v):
    centred = v - jnp.mean(v, axis=1, keepdims=True)
    r = lax.rsqrt(jnp.mean(centred * centred, axis=1, keepdims=True) + EPS)
    return centred * r, r


def norm_back(v, e, gain):
    n, r = norm_parts(v)
    eg = e * gain
    grad = r * (
        eg
        - jnp.mean(eg, axis=1, keepdims=True)
        - n * jnp.mean(eg * n, axis=1, keepdims=True)
    )
    return grad, n


def col_sum(v):
    return jnp.sum(v, axis=0, keepdims=True)


def head_part(v, h):
    lane = lax.broadcasted_iota(jnp.int32, v.shape, 1)
    return jnp.where((lane >= HD * h) & (lane < HD * h + HD), v, jnp.zeros_like(v))


class Place:
    def __init__(self):
        dp = lax.axis_index("dp")
        self.t = t = lax.axis_index("tensor")
        self.z = dp // 8
        self.yl = (dp // 4) % 2
        self.x = dp % 4
        self.c = t % 2
        self.yh = t // 2
        self.t_sib = t + 1 - 2 * self.c
        self.t_part = (t + 2) % 4
        self.t_far = (self.t_sib + 2) % 4
        self.sib = (dp, self.t_sib)
        self.part = (dp, self.t_part)
        self.ypeer = (dp + 4 - 8 * self.yl, t)
        self.dp = dp

    def xpeer(self, j):
        return (self.dp - self.x + (self.x + j) % 4, self.t)

    def zpeer(self, j):
        return (((self.z + j) % 4) * 8 + self.dp % 8, self.t)

    def core_and_x(self, k):
        dp, _ = self.xpeer(k % 4)
        return (dp, self.t if k < 4 else self.t_sib)

    def y_and_z(self, k):
        dp, _ = self.zpeer(k % 4)
        return (dp if k < 4 else dp + 4 - 8 * self.yl, self.t)

    def peers(self):
        return (
            [self.part]
            + [self.core_and_x(k) for k in range(1, 5)]
            + [self.y_and_z(k) for k in range(1, 5)]
        )


def remote(src, dst, send, recv, device):
    return pltpu.make_async_remote_copy(
        src_ref=src,
        dst_ref=dst,
        send_sem=send,
        recv_sem=recv,
        device_id=device,
        device_id_type=MESH,
    )


class Reduction:
    def __init__(self, at, stg, r1, r2, ry, send, recv, free):
        self.at, self.stg, self.r1, self.r2, self.ry = at, stg, r1, r2, ry
        self.send, self.recv, self.free = send, recv, free
        self.big = stg.shape[0] // 4
        self.small = stg.shape[0] // 16

    def axes(self, h):
        at = self.at
        if h == 0:
            return at.x, at.z, at.xpeer, at.zpeer
        return at.z, at.x, at.zpeer, at.xpeer

    def block(self, h, first):
        rows = pl.ds(pl.multiple_of(first * self.big, self.big), self.big)
        return self.stg.at[rows, pl.ds(h * 384, 384)]

    def part(self, h, first, second):
        start = pl.multiple_of(first * self.big + second * self.small, self.small)
        return self.stg.at[pl.ds(start, self.small), pl.ds(h * 384, 384)]

    def copy(self, step, src, dst, device):
        return remote(src, dst, self.send.at[step], self.recv.at[step], device)

    def all_of(self, step):
        ref = (self.r1, self.r2, self.ry, self.r2, self.r1)[step]
        return self.copy(step, ref, ref, self.at.sib)

    def arrived(self, step):
        self.all_of(step).wait_recv()

    def left(self, step):
        self.all_of(step).wait_send()

    def give_back(self, stage):
        self.left(stage)
        for h in (0, 1):
            peer = self.axes(h)[2 + stage]
            for j in (1, 2, 3):
                pl.semaphore_signal(
                    self.free.at[stage], inc=1, device_id=peer(j), device_id_type=MESH
                )

    def start(self):
        for h in (0, 1):
            first, _, peer, _ = self.axes(h)
            for j in (1, 2, 3):
                src = self.block(h, (first + j) % 4)
                self.copy(0, src, self.r1.at[h, j - 1], peer(j)).start()

    def second(self):
        self.arrived(0)
        for h in (0, 1):
            first, second, _, peer = self.axes(h)
            own = self.block(h, first)
            total = own[...].astype(F32)
            for j in (0, 1, 2):
                total = total + self.r1[h, j].astype(F32)
            own[...] = total.astype(BF)
            for j in (1, 2, 3):
                src = self.part(h, first, (second + j) % 4)
                self.copy(1, src, self.r2.at[h, j - 1], peer(j)).start()
        self.give_back(0)

    def third(self):
        self.arrived(1)
        for h in (0, 1):
            first, second, _, _ = self.axes(h)
            own = self.part(h, first, second)
            total = own[...].astype(F32)
            for j in (0, 1, 2):
                total = total + self.r2[h, j].astype(F32)
            own[...] = total.astype(BF)
            self.copy(2, own, self.ry.at[h], self.at.ypeer).start()
        self.give_back(1)

    def fourth(self):
        self.arrived(2)
        self.left(2)
        pl.semaphore_wait(self.free.at[1], 6)
        for h in (0, 1):
            first, second, _, peer = self.axes(h)
            own = self.part(h, first, second)
            own[...] = (own[...].astype(F32) + self.ry[h].astype(F32)).astype(BF)
            for j in (1, 2, 3):
                self.copy(3, own, own, peer(j)).start()

    def fifth(self):
        self.arrived(3)
        pl.semaphore_wait(self.free.at[0], 6)
        for h in (0, 1):
            first, _, peer, _ = self.axes(h)
            own = self.block(h, first)
            for j in (1, 2, 3):
                self.copy(4, own, own, peer(j)).start()

    def finish(self):
        self.arrived(4)

    def drain(self):
        self.left(3)
        self.left(4)


def kernel(
    comm,
    x_hbm,
    cot_hbm,
    wqkv_hbm,
    wout_hbm,
    wup_hbm,
    wdown_hbm,
    flags_hbm,
    mask_hbm,
    bqv_hbm,
    gain1_hbm,
    shift1_hbm,
    bout_hbm,
    gain2_hbm,
    shift2_hbm,
    bup_hbm,
    bdown_hbm,
    res,
    gin,
    stg_u,
    stg_d,
    stg_q,
    small_ref,
    flags_ref,
    mask_ref,
    bqv_ref,
    gain1_ref,
    shift1_ref,
    bout_ref,
    gain2_ref,
    shift2_ref,
    bup_ref,
    bdown_ref,
    x_ref,
    u_ref,
    wqkv,
    wof,
    wup,
    wdown,
    fwup,
    fwdown,
    bias,
    fbias,
    n1,
    q8,
    keys,
    vals,
    att,
    lse,
    mid,
    n2,
    nt2,
    actt,
    own_a,
    own_b,
    s1,
    r1,
    ex,
    mlow,
    gp,
    sc,
    pr,
    ds,
    red1,
    red2,
    redy,
    remy,
    weight,
    sm,
    smp,
    smx,
    smz,
    in_sem,
    a_send,
    a_recv,
    w_send,
    w_recv,
    t_send,
    t_recv,
    x_send,
    x_recv,
    d_send,
    d_recv,
    d_free,
    m_send,
    m_recv,
):
    at = Place()
    c, yh, t = (at.c, at.yh, at.t) if comm else (0, 0, 0)
    ghid = gin
    gpt = nt2.at[0:576]

    def lanes(s, half=None):
        if half is None:
            return pl.ds(pl.multiple_of(s * LEN, LEN), LEN)
        return pl.ds(pl.multiple_of(s * LEN + half * HALF, HALF), HALF)

    def core_rows(core):
        return pl.ds(pl.multiple_of(core * QUART, QUART), QUART)

    def flat(v):
        return v.reshape(-1, v.shape[-1])

    def wout_rows(t, start, count):
        return wof.at[pl.ds(pl.multiple_of(t * 192 + start, 48), count)]

    def wout_block(t):
        return wout_rows(t, 0, 192)

    def att_block(s):
        def block(t):
            return att.at[s, pl.ds(pl.multiple_of(t * 192, 192), 192)]

        block.rows = 192
        return block

    def row_block(ref, s):
        def block(t):
            return ref.at[s, t // 2, t % 2]

        block.rows = QUART
        return block

    def load(i, src, dst):
        return pltpu.make_async_copy(src, dst, in_sem.at[i])

    def load_x(s):
        return load(s, x_hbm.at[s], x_ref.at[s])

    load_wqkv = load(3, wqkv_hbm, wqkv)
    load_wout = load(4, wout_hbm, wout_block(t))
    load_cot = load(5, cot_hbm, u_ref)
    load_up = load(6, wup_hbm, wup)
    load_down = load(7, wdown_hbm, wdown)
    small_loads = [
        load(8 + i, src, dst)
        for i, (src, dst) in enumerate(
            (
                (gain1_hbm, gain1_ref),
                (shift1_hbm, shift1_ref),
                (bqv_hbm, bqv_ref),
                (bup_hbm, bup_ref),
                (flags_hbm, flags_ref),
                (mask_hbm, mask_ref),
                (bout_hbm, bout_ref),
                (gain2_hbm, gain2_ref),
                (shift2_hbm, shift2_ref),
                (bdown_hbm, bdown_ref),
            )
        )
    ]
    load_x(0).start()
    load_wqkv.start()
    if comm:
        barrier = pltpu.get_barrier_semaphore()
        peers = at.peers()
        for peer in peers:
            pl.semaphore_signal(barrier, inc=1, device_id=peer, device_id_type=MESH)
    for copy in small_loads:
        copy.start()
    load_wout.start()
    load_up.start()
    load_down.start()
    load_x(1).start()
    load_x(2).start()
    load_cot.start()
    sm[...] = jnp.zeros_like(sm)
    for copy in small_loads:
        copy.wait()
    bias[...] = jnp.broadcast_to(bup_ref[...].reshape(1, D), (8, D))
    weight[...] = jnp.maximum(flags_ref[...], mask_ref[...]).astype(F32).reshape(2 * SEQS, HALF)

    def fetch_part(i, count):
        first, second = (at.x, at.z) if i == 0 else (at.z, at.x)
        start = (second * 4 + (first if count == 1 else 0)) * 48
        return pl.ds(pl.multiple_of(start, 48), 48 * count)

    def fetch_copy(step, src, dst, device):
        return remote(src, dst, w_send.at[step], w_recv.at[step], device)

    def fetch_y(i):
        if i == 2:
            ref = wout_rows(t, at.x * 48, 48)
            return fetch_copy(0, ref, ref, at.part)
        src, dst = ((wup, fwup), (wdown, fwdown))[i]
        some = fetch_part(i, 1)
        return fetch_copy(1, src.at[some], dst.at[some], at.part)

    def fetch_a(i, j):
        peer = at.zpeer if i == 1 else at.xpeer
        if i == 2:
            ref = wout_rows(at.t_part, at.x * 48, 48)
            return fetch_copy(3, ref, ref, peer(j))
        ref = (fwup, fwdown)[i].at[fetch_part(i, 1)]
        return fetch_copy(4, ref, ref, peer(j))

    def fetch_b(i, j):
        peer = at.xpeer if i == 1 else at.zpeer
        ref = (fwup, fwdown)[i].at[fetch_part(i, 4)]
        return fetch_copy(5, ref, ref, peer(j))

    def fetch_all(step):
        ref = (wof.at[0:48], fwup.at[0:96], fbias, wof.at[0:144], fwup.at[0:288], nt2.at[0:576])[step]
        return fetch_copy(step, ref, ref, at.part)

    def fetch_first(kinds):
        if comm:
            for i in kinds:
                fetch_y(i).start()
            if 0 in kinds:
                fetch_copy(2, bias, fbias, at.part).start()

    def fetch_second(kinds):
        if comm:
            fetch_all(0 if 2 in kinds else 1).wait_recv()
            for i in kinds:
                for j in (1, 2, 3):
                    fetch_a(i, j).start()

    def fetch_third(kinds):
        if comm:
            fetch_all(3 if 2 in kinds else 4).wait_recv()
            for i in kinds:
                if i < 2:
                    for j in (1, 2, 3):
                        fetch_b(i, j).start()

    def fetch_wait():
        if comm:
            fetch_all(2).wait_recv()
            fetch_all(5).wait_recv()

    def fetch_left():
        if comm:
            for step in (0, 1, 2):
                fetch_all(step).wait_send()

    def fetch_drain():
        if comm:
            for step in (3, 4, 5):
                fetch_all(step).wait_send()

    def gather_copy(i, block, kind, t, device):
        ref = block(t)
        return remote(ref, ref, a_send.at[i], a_recv.at[i, kind], device)

    def gather_start(i, block):
        if comm:
            if not isinstance(i, int) or i != 3:
                gather_copy(i, block, 1, at.t, at.part).start()
            gather_copy(i, block, 0, at.t, at.sib).start()

    def gather_forward(i, block):
        if comm:
            if not isinstance(i, int) or i != 3:
                gather_copy(i, block, 1, at.t_part, at.part).wait_recv()
            gather_copy(i, block, 0, at.t_part, at.sib).start()

    def gather_all(i, block, count):
        if block is wout_block:
            ref = wof.at[0 : 192 * count]
        elif block.rows == 192:
            ref = att.at[0, 0 : 192 * count]
        else:
            ref = n1.at[0, 0 : QUART * count]
        return remote(ref, ref, a_send.at[i], a_recv.at[i, 0], at.sib)

    def gather_wait(i, block):
        if comm:
            gather_all(i, block, 2).wait_recv()

    def gather_drain(i, block):
        if comm:
            gather_all(i, block, 2 if block is wout_block else 3).wait_send()

    def core_copy(k, s):
        return remote(s1.at[k, s - 1], r1.at[k, s - 1], t_send.at[k, s - 1], t_recv.at[k, s - 1], at.sib)

    def core_sum(k, s, own):
        if comm:
            core_copy(k, s).wait()
        return own[s, core_rows(c), :] + r1[k, s - 1].astype(F32)

    def slot(kind, i):
        if isinstance(i, int) and i >= SEQS:
            return ex.at[kind, i - SEQS]
        rows = pl.ds(pl.multiple_of(i * HALF, HALF), HALF)
        if kind % 2 == 0:
            return actt.at[rows, pl.ds(kind // 2 * D, D)]
        return (wup, wdown)[kind // 2].at[rows]

    def chip_copy(i):
        return remote(slot(0, i), slot(1, i), x_send.at[0, i], x_recv.at[0, i], at.sib)

    def group_copy(i):
        return remote(slot(2, i), slot(3, i), x_send.at[1, i], x_recv.at[1, i], at.part)

    def share_copy(i, ref, s, core):
        some = ref.at[s, :, core]
        return remote(some, some, x_send.at[2, i], x_recv.at[2, i], at.sib)

    def chip_sum(i, own):
        if comm:
            chip_copy(i).wait()
        slot(2, i)[...] = (own[...] + slot(1, i)[...].astype(F32)).astype(BF)
        if comm:
            group_copy(i).start()

    def group_arrived(i):
        if comm:
            group_copy(i).wait()

    def group_sum(i, piece):
        return slot(2, i)[piece, :].astype(F32) + slot(3, i)[piece, :].astype(F32)

    def share(i, ref, s):
        if comm:
            share_copy(i, ref, s, c).start()

    def share_wait(i, ref, s):
        if comm:
            share_copy(i, ref, s, 1 - c).wait_recv()

    def core_part(v, core):
        return jnp.where(core == 0, v[:QUART], v[QUART:])

    gain1, shift1, gain2, shift2, b_out, b_down = (
        ref[...].reshape(1, D)
        for ref in (gain1_ref, shift1_ref, gain2_ref, shift2_ref, bout_ref, bdown_ref)
    )

    def add_small(row, value):
        sm[row : row + 1, :] += value

    def project(s):
        load_x(s).wait()
        for half in range(2):
            n, _r = norm_parts(flat(x_ref[s, half]).astype(F32))
            n1[s, HALF * half : HALF * half + HALF, :] = (n * gain1 + shift1).astype(BF)
        normed = n1[s]
        q = (dot(normed, wqkv[0], NT) + bqv_ref[0:1, :]).astype(BF) * SCALE
        q8[s] = q
        k = dot(normed, wqkv[1], NT).astype(BF)
        keys[s] = k
        v = (dot(normed, wqkv[2], NT) + bqv_ref[1:2, :]).astype(BF)
        vals[s] = v

    def attend(s):
        q, k, vt = q8[s], keys[s], vals[s].T
        block = att_block(s)(t)
        for h in range(3):
            sc[...] = dot(head_part(k, h), q, NT)
            for part in range(4):
                cols = slice(part * 128, part * 128 + 128)
                scores = sc[:, cols]
                top = jnp.max(scores, axis=0, keepdims=True)
                e = jnp.exp(scores - top)
                total = col_sum(e)
                lse[3 * s + h, :, cols] = top + jnp.log(total)
                pr[:, cols] = (e * (1.0 / total)).astype(BF)
            mixed = dot(vt[HD * h : HD * h + HD], pr[...], NN)
            block[HD * h : HD * h + HD, :] = mixed.astype(BF)
        gather_start(s, att_block(s))

    def weigh(i, _):
        same = lax.broadcasted_iota(jnp.int32, (HALF, HALF), 0) == lax.broadcasted_iota(
            jnp.int32, (HALF, HALF), 1
        )
        diagonal = jnp.where(same, weight[pl.ds(i, 1), :], 0.0).astype(BF)
        rows = dot(diagonal, flat(u_ref[i // 2, i % 2]), NN).astype(BF)
        u_ref[i // 2, i % 2] = rows.reshape(2, QUART, D)
        return 0

    def hidden_units(normed, up, w_up, b_up, w_down):
        acts, grads = [], []
        for i in range(2):
            some = slice(i * 384, i * 384 + 384)
            v = dot(normed, w_up[:, some], NN) + b_up[:, some]
            back = dot(up, w_down[some, :], NT)
            square = v * v
            th = jnp.tanh(v * (GELU_A + (GELU_A * GELU_B) * square))
            cdf = 0.5 + 0.5 * th
            inner = v * (0.5 * GELU_A + (1.5 * GELU_A * GELU_B) * square)
            acts.append((v * cdf).astype(BF))
            grads.append(back * (cdf + inner * (1.0 - th * th)))
        total = jnp.concatenate([col_sum(grad) for grad in grads], axis=1)
        grad = jnp.concatenate([grad.astype(BF) for grad in grads], axis=1)
        return jnp.concatenate(acts, axis=1), grad, total

    def feed(s, between):
        gather_wait(s, att_block(s))
        for own in (False, True):
            half = yh if own else 1 - yh
            some = lanes(s, half)
            cols = pl.ds(pl.multiple_of(half * HALF, HALF), HALF)
            middle = flat(x_ref[s, half]).astype(F32) + dot(att[s, :, cols], wof[...], TN) + b_out
            n, _r = norm_parts(middle)
            normed = (n * gain2 + shift2).astype(BF)
            nt2[:, some] = normed.T
            act, grad, total = hidden_units(normed, flat(u_ref[s, half]), wup, bias[0:1, :], wdown)
            add_small(BUP, total)
            actt[:, some] = act.T
            ghid[s, half] = grad.reshape(2, QUART, D)
            if own:
                between(1)
            if isinstance(s, int):
                piece = pl.ds(pl.multiple_of(half * QUART, QUART), QUART)
                mid[s, piece, :] = core_part(middle, c)
                for k, (ref, total) in enumerate(
                    ((own_a, dot(grad, wup[...], NT)), (own_b, dot(act, wdown[...], NN)))
                ):
                    ref[s, piece, :] = core_part(total, c)
                    slot(0, 3 + k)[piece, :] = core_part(total, 1 - c).astype(BF)
            elif own:
                mid[s] = middle
                n2[s - 1] = normed
                own_a[s] = dot(grad, wup[...], NT)
                own_b[s] = dot(act, wdown[...], NN)
            if not own:
                between(0)
        if isinstance(s, int) and comm:
            chip_copy(3).start()
            chip_copy(4).start()

    def feed_more(s):
        act, grad, _ = hidden_units(n2[s - 1], flat(u_ref[s, yh]), fwup, fbias[0:1, :], fwdown)
        own_a[s] += dot(grad, fwup[...], NT)
        own_b[s] += dot(act, fwdown[...], NN)
        for k, ref in enumerate((own_a, own_b)):
            s1[k, s - 1] = ref[s, core_rows(1 - c), :].astype(BF)
            if comm:
                core_copy(k, s).start()

    def middle_back(s):
        e = core_sum(0, s, own_a)
        grad, n = norm_back(mid[s, core_rows(c), :], e, gain2)
        add_small(GAIN2, col_sum(e * n))
        add_small(SHIFT2, col_sum(e))
        up = u_ref[s, yh, c].astype(F32)
        grad = up + grad
        add_small(BOUT, col_sum(grad))
        add_small(BDOWN, col_sum(up))
        mlow[s, yh, c] = grad.astype(BF)
        gather_start(4 + s, row_block(mlow, s))

    def middle_back_first():
        group_arrived(3)
        for half in range(2):
            piece = slice(half * QUART, half * QUART + QUART)
            e = group_sum(3, piece)
            grad, n = norm_back(mid[0, piece, :], e, gain2)
            up = u_ref[0, half, c].astype(F32)
            grad = up + grad
            mlow[0, half, c] = grad.astype(BF)
            for row, v in ((GAIN2, e * n), (SHIFT2, e), (BOUT, grad), (BDOWN, up)):
                add_small(row, jnp.where(yh == half, col_sum(v), 0.0))
        share(3, mlow, 0)

    def output_rows_first():
        group_arrived(4)
        for half in range(2):
            piece = slice(half * QUART, half * QUART + QUART)
            total = mid[0, piece, :] + group_sum(4, piece) + b_down
            res[0, half, c] = total.astype(BF)
        share(4, res, 0)

    def output_rows(s):
        total = mid[s, core_rows(c), :] + core_sum(1, s, own_b) + b_down
        res[s, yh, c] = total.astype(BF)
        gather_start(7 + s, row_block(res, s))

    def reduction(i, ref, wide):
        if wide:
            r1, r2, ry = red1.at[i], red2.at[i], redy.at[i]
        else:
            j = i - 2
            r1 = red1.at[0, :, :, pl.ds(j * 64, 64)]
            r2 = red2.at[0, :, :, pl.ds(j * 16, 16)]
            ry = remy.at[j]
        return Reduction(at, ref, r1, r2, ry, d_send.at[i], d_recv.at[i], d_free.at[i])

    d_up, d_down = reduction(0, stg_u, True), reduction(1, stg_d, True)
    d_att = [reduction(2 + i, stg_q.at[pl.ds(i * HALF, HALF)], False) for i in range(3)]

    def reduce_step(name, which):
        if comm:
            getattr(which, name)()

    def stage(stg, start, count, value):
        stg[pl.ds(start, count), :] = value.astype(BF)

    def up_grads(i, _):
        start = pl.multiple_of(i * HALF, HALF)
        some = pl.ds(start, HALF)
        stage(stg_u, start, HALF, dot(nt2[some, :], flat(ghid[...]), NN))
        return 0

    def down_grads(i, _):
        start = pl.multiple_of(i * HALF, HALF)
        some = pl.ds(start, HALF)
        stage(stg_d, start, HALF, dot(actt[some, :], flat(u_ref[...]), NN))
        return 0

    def qkv_grads(start, count):
        stage(stg_q, start, count, dot(gpt[start : start + count, :], flat(n1[...]), NN))

    def out_grads():
        total = jnp.zeros((192, D), F32)
        for s in range(SEQS):
            total += dot(att_block(s)(t)[...], flat(mlow[s]), NN)
        stage(stg_q, 576, 192, total)

    def attend_back(s, between):
        some_lanes = lanes(s)
        mixed = dot(flat(mlow[s]), wout_block(t)[...], NT).astype(BF)
        q, k, v = q8[s], keys[s], vals[s]
        kt = k.T
        grad_k = jnp.zeros((LEN, 192), F32)
        grad_v = jnp.zeros((LEN, 192), F32)
        for h in range(3):
            sc[...] = dot(head_part(k, h), q, NT)
            back = dot(head_part(v, h), mixed, NT)
            some = slice(HD * h, HD * h + HD)
            for part in range(4):
                cols = slice(part * 128, part * 128 + 128)
                p = jnp.exp(sc[:, cols] - lse[3 * s + h, :, cols])
                pr[:, cols] = p.astype(BF)
                gp_part = back[:, cols]
                total = col_sum(gp_part * p)
                ds[:, cols] = (p * (gp_part - total)).astype(BF)
            grad_v += dot(pr[...], head_part(mixed, h), NN)
            grad_k += dot(ds[...], head_part(q, h), NN)
            gpt[some, some_lanes] = (dot(kt[some], ds[...], NN) * SCALE).astype(BF)
            between(h)
        grad_q = gpt[0:192, some_lanes].T
        grad_k = grad_k.astype(BF)
        grad_v = grad_v.astype(BF)
        gpt[192:384, some_lanes] = grad_k.T
        gpt[384:576, some_lanes] = grad_v.T
        for i, grad in enumerate((grad_q, grad_k, grad_v)):
            gp[i] = grad.reshape(2, 2, QUART, 192)
        sm[BQV : BQV + 1, 0:192] += col_sum(grad_q.astype(F32))
        sm[BQV : BQV + 1, 256:448] += col_sum(grad_v.astype(F32))
        for own in (False, True):
            core = c if own else 1 - c
            total = dot(flat(gp[0, :, core]), wqkv[0], NN)
            total += dot(flat(gp[1, :, core]), wqkv[1], NN)
            total += dot(flat(gp[2, :, core]), wqkv[2], NN)
            if own:
                own_a[s] = total
            else:
                slot(0, s)[...] = total.astype(BF)
                if comm:
                    chip_copy(s).start()

    def input_back(s):
        group_arrived(s)
        for half in range(2):
            e = group_sum(s, slice(half * QUART, half * QUART + QUART))
            grad, n = norm_back(x_ref[s, half, c].astype(F32), e, gain1)
            add_small(GAIN1, col_sum(e * n))
            add_small(SHIFT1, col_sum(e))
            gin[s, half, c] = (mlow[s, half, c].astype(F32) + grad).astype(BF)
        share(s, gin, s)

    def small_copy(i, slots, slot, device):
        ref = slots.at[slot]
        return remote(ref, ref, m_send.at[i], m_recv.at[i], device)

    def small_row():
        return lax.broadcasted_iota(jnp.int32, (8, D), 0)

    def small_part():
        smp[yh] = sm[...]
        if comm:
            small_copy(0, smp, yh, at.part).start()

    def small_all(i, slots):
        return remote(slots.at[0:7], slots.at[0:7], m_send.at[i], m_recv.at[i], at.sib)

    def first_slot():
        return at.c * 4 + at.x

    def second_slot():
        return at.yl * 4 + at.z

    def small_first():
        small_copy(0, smp, 1 - yh, at.part).wait_recv()
        row = small_row()
        smx[first_slot()] = jnp.where((row >= GAIN2) & (row < BUP), smp[0] + smp[1], sm[...])
        for k in range(1, 8):
            small_copy(1, smx, first_slot(), at.core_and_x(k)).start()

    def small_second():
        small_all(1, smx).wait_recv()
        cores = [
            (smx[4 * i] + smx[4 * i + 1]) + (smx[4 * i + 2] + smx[4 * i + 3]) for i in (0, 1)
        ]
        mine = jnp.where(c == 0, cores[0], cores[1])
        smz[second_slot()] = jnp.where(small_row() < BUP, cores[0] + cores[1], mine)
        for k in range(1, 8):
            small_copy(2, smz, second_slot(), at.y_and_z(k)).start()

    def small_end():
        small_all(2, smz).wait_recv()
        total = smz[0]
        for i in range(1, 8):
            total = total + smz[i]
        small_ref[...] = total

    def small_drain():
        small_copy(0, smp, yh, at.part).wait_send()
        small_all(1, smx).wait_send()
        small_all(2, smz).wait_send()

    load_wqkv.wait()
    project(0)
    load_wout.wait()
    load_up.wait()
    load_down.wait()
    if comm:
        pl.semaphore_wait(barrier, len(peers))
    fetch_first((2,))
    gather_start(3, wout_block)

    def attend_all(s, _):
        @pl.when(s > 0)
        def _():
            project(s)

        @pl.when(s == 1)
        def _():
            fetch_second((2,))

        attend(s)

        @pl.when(s == 0)
        def _():
            fetch_first((0, 1))

        return 0

    lax.fori_loop(0, SEQS, attend_all, 0)
    load_cot.wait()
    lax.fori_loop(0, 2, weigh, 0)
    fetch_third((2,))
    gather_forward(3, wout_block)
    lax.fori_loop(2, 2 * SEQS, weigh, 0)
    gather_forward(0, att_block(0))
    fetch_second((0, 1))
    gather_wait(3, wout_block)

    def feed_first(slot):
        if slot == 1:
            gather_forward(1, att_block(1))

    feed(0, feed_first)
    fetch_third((0, 1))

    def feed_all(s, _):
        def between(slot):
            @pl.when(s == 1)
            def _():
                if slot == 0:
                    chip_sum(3, own_a.at[0])
                    chip_sum(4, own_b.at[0])
                else:
                    gather_forward(2, att_block(2))

        feed(s, between)
        return 0

    lax.fori_loop(1, SEQS, feed_all, 0)
    fetch_left()
    lax.fori_loop(0, 3, up_grads, 0)
    reduce_step("start", d_up)
    lax.fori_loop(0, 3, down_grads, 0)
    middle_back_first()
    fetch_wait()
    feed_more(1)
    feed_more(2)
    middle_back(1)
    fetch_drain()
    gather_drain(3, wout_block)
    for s in range(SEQS):
        gather_drain(s, att_block(s))
    middle_back(2)
    small_part()
    share_wait(3, mlow, 0)

    def attend_back_all(s, _):
        def between(h):
            if h == 0:

                @pl.when(s == 0)
                def _():
                    reduce_step("second", d_up)
                    reduce_step("start", d_down)

                @pl.when(s == 2)
                def _():
                    reduce_step("fifth", d_up)
                    chip_sum(1, own_a.at[1])

            if h == 1:

                @pl.when(s == 0)
                def _():
                    output_rows_first()

                @pl.when(s == 1)
                def _():
                    gather_forward(6, row_block(mlow, 2))
                    reduce_step("fourth", d_up)

                @pl.when(s == 2)
                def _():
                    reduce_step("third", d_down)

            if h == 2:

                @pl.when(s == 1)
                def _():
                    reduce_step("second", d_down)

        attend_back(s, between)

        @pl.when(s == 0)
        def _():
            gather_forward(5, row_block(mlow, 1))
            reduce_step("third", d_up)
            chip_sum(0, own_a.at[0])
            gather_wait(5, row_block(mlow, 1))

        @pl.when(s == 1)
        def _():
            gather_wait(6, row_block(mlow, 2))

        return 0

    lax.fori_loop(0, SEQS, attend_back_all, 0)
    qkv_grads(0, HALF)
    reduce_step("start", d_att[0])
    qkv_grads(HALF, HALF)
    reduce_step("start", d_att[1])
    qkv_grads(2 * HALF, 64)
    out_grads()
    reduce_step("start", d_att[2])
    chip_sum(2, own_a.at[2])
    reduce_step("fourth", d_down)
    input_back(0)
    for s in (1, 2):
        gather_drain(4 + s, row_block(mlow, s))
    reduce_step("second", d_att[0])
    reduce_step("second", d_att[1])
    reduce_step("second", d_att[2])
    reduce_step("fifth", d_down)
    input_back(1)
    for part in d_att:
        reduce_step("third", part)
    output_rows(1)
    input_back(2)
    if comm:
        small_first()
    reduce_step("fourth", d_att[0])
    reduce_step("fourth", d_att[1])
    reduce_step("fourth", d_att[2])
    output_rows(2)
    for s in range(SEQS):
        share_wait(s, gin, s)
    share_wait(4, res, 0)
    reduce_step("fifth", d_att[0])
    if comm:
        small_second()
    reduce_step("fifth", d_att[1])
    reduce_step("fifth", d_att[2])
    gather_forward(8, row_block(res, 1))
    reduce_step("finish", d_up)
    reduce_step("drain", d_up)
    gather_forward(9, row_block(res, 2))
    reduce_step("finish", d_down)
    reduce_step("drain", d_down)
    if comm:
        for i, ref, s in ((0, gin, 0), (1, gin, 1), (2, gin, 2), (3, mlow, 0), (4, res, 0)):
            share_copy(i, ref, s, c).wait_send()
    for s in (1, 2):
        gather_wait(7 + s, row_block(res, s))
        gather_drain(7 + s, row_block(res, s))
    if comm:
        small_end()
        small_drain()
    else:
        small_ref[...] = sm[...]
    for part in d_att:
        reduce_step("finish", part)
        reduce_step("drain", part)


def layer(comm, x, cot, *rest):
    rows = (SEQS, 2, 2, QUART, D)
    half = (SEQS, HALF, D)
    dma = pltpu.SemaphoreType.DMA
    scratch = [
        pltpu.VMEM((ROWS,), jnp.int32),
        pltpu.VMEM((ROWS,), jnp.int32),
        pltpu.VMEM((2, 192), F32),
        pltpu.VMEM((D,), F32),
        pltpu.VMEM((D,), F32),
        pltpu.VMEM((D,), F32),
        pltpu.VMEM((D,), F32),
        pltpu.VMEM((D,), F32),
        pltpu.VMEM((D,), F32),
        pltpu.VMEM((D,), F32),
        pltpu.VMEM(rows, BF),
        pltpu.VMEM(rows, BF),
        pltpu.VMEM((3, 192, D), BF),
        pltpu.VMEM((D, D), BF),
        pltpu.VMEM((D, D), BF),
        pltpu.VMEM((D, D), BF),
        pltpu.VMEM((D, D), BF),
        pltpu.VMEM((D, D), BF),
        pltpu.VMEM((8, D), F32),
        pltpu.VMEM((8, D), F32),
        pltpu.VMEM((SEQS, LEN, D), BF),
        pltpu.VMEM((SEQS, LEN, 192), BF),
        pltpu.VMEM((SEQS, LEN, 192), BF),
        pltpu.VMEM((SEQS, LEN, 192), BF),
        pltpu.VMEM((SEQS, D, LEN), BF),
        pltpu.VMEM((3 * SEQS, 1, LEN), F32),
        pltpu.VMEM(half, F32),
        pltpu.VMEM((SEQS - 1, HALF, D), BF),
        pltpu.VMEM((D, ROWS), BF),
        pltpu.VMEM((D, ROWS), BF),
        pltpu.VMEM(half, F32),
        pltpu.VMEM(half, F32),
        pltpu.VMEM((2, SEQS - 1, QUART, D), BF),
        pltpu.VMEM((2, SEQS - 1, QUART, D), BF),
        pltpu.VMEM((4, 2, HALF, D), BF),
        pltpu.VMEM(rows, BF),
        pltpu.VMEM((3, 2, 2, QUART, 192), BF),
        pltpu.VMEM((LEN, LEN), F32),
        pltpu.VMEM((LEN, LEN), BF),
        pltpu.VMEM((LEN, LEN), BF),
        pltpu.VMEM((2, 2, 3, 192, 384), BF),
        pltpu.VMEM((2, 2, 3, 48, 384), BF),
        pltpu.VMEM((2, 2, 48, 384), BF),
        pltpu.VMEM((3, 2, 16, 384), BF),
        pltpu.VMEM((2 * SEQS, HALF), F32),
        pltpu.VMEM((8, D), F32),
        pltpu.VMEM((2, 8, D), F32),
        pltpu.VMEM((8, 8, D), F32),
        pltpu.VMEM((8, 8, D), F32),
        dma((18,)),
        dma((10,)),
        dma((10, 2)),
        dma((6,)),
        dma((6,)),
        dma((2, SEQS - 1)),
        dma((2, SEQS - 1)),
        dma((3, 5)),
        dma((3, 5)),
        dma((5, 5)),
        dma((5, 5)),
        pltpu.SemaphoreType.REGULAR((5, 2)),
        dma((3,)),
        dma((3,)),
    ]
    anywhere = pl.BlockSpec(memory_space=pl.ANY)
    vmem = pl.BlockSpec(memory_space=pltpu.VMEM)
    return pl.pallas_call(
        functools.partial(kernel, comm),
        out_shape=(
            pltpu.VMEM(rows, BF),
            pltpu.VMEM(rows, BF),
            pltpu.VMEM((D, D), BF),
            pltpu.VMEM((D, D), BF),
            pltpu.VMEM((D, D), BF),
            pltpu.VMEM((8, D), F32),
        ),
        in_specs=[anywhere] * 16,
        out_specs=(vmem,) * 6,
        scratch_shapes=scratch,
        compiler_params=pltpu.CompilerParams(
            collective_id=0 if comm else None,
            has_side_effects=True,
            vmem_limit_bytes=55 * 2**20,
        ),
        cost_estimate=pl.CostEstimate(
            flops=20 * 10**9, bytes_accessed=20 * 10**6, transcendentals=10**7
        ),
        name="layer",
    )(x.reshape(rows), cot.reshape(rows), *rest)


def results(out, gin, g_up, g_down, g_qkv, small):
    def kernel(out, gin, up, down, qkv, small, *rest):
        (out_to, gin_to, qkv_to, out_w_to, up_to, down_to, bqv_to), rest = rest[:7], rest[7:]
        vectors, (wide, sem) = rest[:7], rest[7:]
        copies = []

        def start(i, src, dst):
            copy = pltpu.make_async_copy(src, dst, sem.at[i])
            copy.start()
            copies.append(copy)

        start(0, out, out_to)
        start(1, gin, gin_to)
        for i, (src, first, rows, dst) in enumerate(
            (
                (up, 0, D, up_to),
                (down, 0, D, down_to),
                (qkv, 0, 576, qkv_to),
                (qkv, 576, 192, out_w_to),
            )
        ):
            at = (0, D, 2 * D, 2 * D + 576)[i]
            wide[at : at + rows, :] = src[first : first + rows, :].astype(F32)
            start(2 + i, wide.at[pl.ds(at, rows)], dst)
        for row, ref in zip((GAIN1, SHIFT1, BOUT, GAIN2, SHIFT2, BUP, BDOWN), vectors):
            ref[...] = small[row : row + 1, :].reshape(D)
        bqv_to[0:1, :] = small[BQV : BQV + 1, 0:192]
        bqv_to[1:2, :] = small[BQV : BQV + 1, 256:448]
        for copy in copies:
            copy.wait()

    anywhere = pl.BlockSpec(memory_space=pl.ANY)
    vmem = pl.BlockSpec(memory_space=pltpu.VMEM)

    def shape(*dims, dtype=F32):
        return jax.ShapeDtypeStruct(dims, dtype)

    return pl.pallas_call(
        kernel,
        out_shape=(
            shape(*out.shape, dtype=BF),
            shape(*gin.shape, dtype=BF),
            shape(576, D),
            shape(192, D),
            shape(D, D),
            shape(D, D),
            shape(2, 192),
        )
        + (shape(D),) * 7,
        in_specs=[vmem] * 6,
        out_specs=(anywhere,) * 6 + (vmem,) * 8,
        scratch_shapes=[pltpu.VMEM((3 * D, D), F32), pltpu.SemaphoreType.DMA((6,))],
        compiler_params=pltpu.CompilerParams(vmem_limit_bytes=12 * 2**20),
        name="results",
    )(
        *(
            pltpu.with_memory_space_constraint(v, pltpu.VMEM)
            for v in (out, gin, g_up, g_down, g_qkv, small)
        )
    )


def shards(
    layer_input,
    flags,
    loss_mask,
    cotangent,
    gain_one,
    shift_one,
    w_qkv,
    b_qv,
    w_out,
    b_out,
    gain_two,
    shift_two,
    w_up,
    b_up,
    w_down,
    b_down,
    comm=True,
):
    parts = layer(
        comm,
        layer_input,
        cotangent,
        w_qkv.transpose(0, 2, 1),
        w_out,
        w_up,
        w_down,
        flags,
        loss_mask,
        b_qv,
        gain_one,
        shift_one,
        b_out,
        gain_two,
        shift_two,
        b_up,
        b_down,
    )
    out, gin, g_qkv, g_out, g_up, g_down, g_bqv, *vectors = results(*parts)
    g_gain1, g_shift1, g_bout, g_gain2, g_shift2, g_bup, g_bdown = vectors
    return (
        out.reshape(ROWS, D),
        gin.reshape(ROWS, D),
        g_gain1,
        g_shift1,
        g_qkv.reshape(3, 192, D).transpose(0, 2, 1),
        g_bqv,
        g_out,
        g_bout,
        g_gain2,
        g_shift2,
        g_up,
        g_bup,
        g_down,
        g_bdown,
    )


def solution(mesh):
    in_specs = (
        P("dp", None),
        P("dp"),
        P("dp"),
        P("dp", None),
        P(),
        P(),
        P(None, None, "tensor"),
        P(None, "tensor"),
        P("tensor", None),
        P(),
        P(),
        P(),
        P(None, "tensor"),
        P("tensor"),
        P("tensor", None),
        P(),
    )
    out_specs = (
        P("dp", None),
        P("dp", None),
        P(),
        P(),
        P(None, None, "tensor"),
        P(None, "tensor"),
        P("tensor", None),
        P(),
        P(),
        P(),
        P(None, "tensor"),
        P("tensor"),
        P("tensor", None),
        P(),
    )
    return jax.shard_map(shards, mesh=mesh, in_specs=in_specs, out_specs=out_specs, check_vma=False)
```

time: 121 us -> 109 us (0.901)
  other arithmetic: 5.94 us -> 0 us
  local copies, waits for them, and re-layouts: 3.53 us -> 0 us
  Pallas kernels: 110 us -> 108 us
    pallas_call x1, Pallas kernels: 110 us -> 103 us  [layer(): pl.pallas_call(functools.partial(kernel, comm), out_shape=(pltpu.VMEM(row...]
    convert_element_type x4 -> x0, other arithmetic: 5.36 us -> none  [the longest x1 1.58 us: shards(): g_up.astype(F32)]
    pallas_call x0 -> x1, Pallas kernels: none -> 4.99 us  [results(): pl.pallas_call(kernel, out_shape=(shape(*out.shape, dtype=BF), shape(*gin...]
    unnamed x2 -> x0, local copies, waits for them, and re-layouts: 2.81 us -> none
where the time goes in v3:
time: 109 us
  Pallas kernels  108 us (99%)
    pallas_call x1, Pallas kernels, layer(): pl.pallas_call(functools.partial(kernel, comm), out_shape=(pltpu.VMEM(row...  103 us
    pallas_call x1, Pallas kernels, results(): pl.pallas_call(kernel, out_shape=(shape(*out.shape, dtype=BF), shape(*gin...  4.99 us

profile of v3, /device:TPU:0, one launch (start us, length us, event | category | flops | bytes accessed | tf_op | source)
XLA Modules:
  0.0 108.7 jit_solution(5972361467669873192)
XLA Ops:
  0.7 102.9 %layer.1 = (bf16[3,2,2,128,768]{4,3,2,1,0:T(8,128)(2,1)S(1)}, bf16[3,2,2,128,768]{4,3,2,1,0:T(8,128)(2,1)S(1)}, bf16[768,768]{1,0:T(8,128)(2,1)S(1)}, bf16[768,7...) custom-call(bf16[3,2,2,128,768]{4,3,2,1,0:T(8,128)(2,1)} %bitcast.8, ...), custom_call_target="tpu_custom_call" | custom-call | flops 20000000000 | bytes 20000000 | tf_op jit(solution)/shard_map/layer/pallas_call | solution.py:1086
  103.5 5.0 %results.1 = (bf16[3,2,2,128,768]{4,3,2,1,0:T(8,128)(2,1)}, bf16[3,2,2,128,768]{4,3,2,1,0:T(8,128)(2,1)}, f32[576,768]{1,0:T(8,128)}, f32[192,768]{1,0:T(8,128)}...) custom-call(bf16[3,2,2,128,768]{4,3,2,1,0:T(8,128)(2,1)S(1)} %get-tu, ...), custom_call_target="tpu_custom_call" | custom-call | tf_op jit(solution)/shard_map/results/pallas_call | solution.py:1148

commit v4 on v3

--- a/solution.py
+++ b/solution.py
@@ -522,12 +522,10 @@
         if comm:
             group_copy(i).start()
 
-    def group_arrived(i):
+    def group_sum(i):
         if comm:
             group_copy(i).wait()
-
-    def group_sum(i, piece):
-        return slot(2, i)[piece, :].astype(F32) + slot(3, i)[piece, :].astype(F32)
+        return slot(2, i)[...].astype(F32) + slot(3, i)[...].astype(F32)
 
     def share(i, ref, s):
         if comm:
@@ -539,6 +537,9 @@
 
     def core_part(v, core):
         return jnp.where(core == 0, v[:QUART], v[QUART:])
+
+    def chip_rows_sum(v):
+        return jnp.where(yh == 0, col_sum(v[:QUART]), col_sum(v[QUART:]))
 
     gain1, shift1, gain2, shift2, b_out, b_down = (
         ref[...].reshape(1, D)
@@ -588,20 +589,13 @@
         return 0
 
     def hidden_units(normed, up, w_up, b_up, w_down):
-        acts, grads = [], []
-        for i in range(2):
-            some = slice(i * 384, i * 384 + 384)
-            v = dot(normed, w_up[:, some], NN) + b_up[:, some]
-            back = dot(up, w_down[some, :], NT)
-            square = v * v
-            th = jnp.tanh(v * (GELU_A + (GELU_A * GELU_B) * square))
-            cdf = 0.5 + 0.5 * th
-            inner = v * (0.5 * GELU_A + (1.5 * GELU_A * GELU_B) * square)
-            acts.append((v * cdf).astype(BF))
-            grads.append(back * (cdf + inner * (1.0 - th * th)))
-        total = jnp.concatenate([col_sum(grad) for grad in grads], axis=1)
-        grad = jnp.concatenate([grad.astype(BF) for grad in grads], axis=1)
-        return jnp.concatenate(acts, axis=1), grad, total
+        v = dot(normed, w_up[...], NN) + b_up
+        back = dot(up, w_down[...], NT)
+        square = v * v
+        th = jnp.tanh(v * (GELU_A + (GELU_A * GELU_B) * square))
+        cdf = 0.5 + 0.5 * th
+        inner = v * (0.5 * GELU_A + (1.5 * GELU_A * GELU_B) * square)
+        return (v * cdf).astype(BF), back * (cdf + inner * (1.0 - th * th))
 
     def feed(s, between):
         gather_wait(s, att_block(s))
@@ -613,8 +607,9 @@
             n, _r = norm_parts(middle)
             normed = (n * gain2 + shift2).astype(BF)
             nt2[:, some] = normed.T
-            act, grad, total = hidden_units(normed, flat(u_ref[s, half]), wup, bias[0:1, :], wdown)
-            add_small(BUP, total)
+            act, grad = hidden_units(normed, flat(u_ref[s, half]), wup, bias[0:1, :], wdown)
+            add_small(BUP, col_sum(grad))
+            grad = grad.astype(BF)
             actt[:, some] = act.T
             ghid[s, half] = grad.reshape(2, QUART, D)
             if own:
@@ -639,8 +634,8 @@
             chip_copy(4).start()
 
     def feed_more(s):
-        act, grad, _ = hidden_units(n2[s - 1], flat(u_ref[s, yh]), fwup, fbias[0:1, :], fwdown)
-        own_a[s] += dot(grad, fwup[...], NT)
+        act, grad = hidden_units(n2[s - 1], flat(u_ref[s, yh]), fwup, fbias[0:1, :], fwdown)
+        own_a[s] += dot(grad.astype(BF), fwup[...], NT)
         own_b[s] += dot(act, fwdown[...], NN)
         for k, ref in enumerate((own_a, own_b)):
             s1[k, s - 1] = ref[s, core_rows(1 - c), :].astype(BF)
@@ -660,24 +655,20 @@
         gather_start(4 + s, row_block(mlow, s))
 
     def middle_back_first():
-        group_arrived(3)
-        for half in range(2):
-            piece = slice(half * QUART, half * QUART + QUART)
-            e = group_sum(3, piece)
-            grad, n = norm_back(mid[0, piece, :], e, gain2)
-            up = u_ref[0, half, c].astype(F32)
-            grad = up + grad
-            mlow[0, half, c] = grad.astype(BF)
-            for row, v in ((GAIN2, e * n), (SHIFT2, e), (BOUT, grad), (BDOWN, up)):
-                add_small(row, jnp.where(yh == half, col_sum(v), 0.0))
+        e = group_sum(3)
+        grad, n = norm_back(mid[0], e, gain2)
+        add_small(GAIN2, chip_rows_sum(e * n))
+        add_small(SHIFT2, chip_rows_sum(e))
+        up = flat(u_ref[0, :, c]).astype(F32)
+        grad = up + grad
+        add_small(BOUT, chip_rows_sum(grad))
+        add_small(BDOWN, chip_rows_sum(up))
+        mlow[0, :, c] = grad.astype(BF).reshape(2, QUART, D)
         share(3, mlow, 0)
 
     def output_rows_first():
-        group_arrived(4)
-        for half in range(2):
-            piece = slice(half * QUART, half * QUART + QUART)
-            total = mid[0, piece, :] + group_sum(4, piece) + b_down
-            res[0, half, c] = total.astype(BF)
+        total = mid[0] + group_sum(4) + b_down
+        res[0, :, c] = total.astype(BF).reshape(2, QUART, D)
         share(4, res, 0)
 
     def output_rows(s):
@@ -770,14 +761,40 @@
                     chip_copy(s).start()
 
     def input_back(s):
-        group_arrived(s)
-        for half in range(2):
-            e = group_sum(s, slice(half * QUART, half * QUART + QUART))
-            grad, n = norm_back(x_ref[s, half, c].astype(F32), e, gain1)
-            add_small(GAIN1, col_sum(e * n))
-            add_small(SHIFT1, col_sum(e))
-            gin[s, half, c] = (mlow[s, half, c].astype(F32) + grad).astype(BF)
+        e = group_sum(s)
+        grad, n = norm_back(flat(x_ref[s, :, c]).astype(F32), e, gain1)
+        add_small(GAIN1, chip_rows_sum(e * n))
+        add_small(SHIFT1, chip_rows_sum(e))
+        total = flat(mlow[s, :, c]).astype(F32) + grad
+        gin[s, :, c] = total.astype(BF).reshape(2, QUART, D)
         share(s, gin, s)
+
+    LAST = SEQS - 1
+
+    def last_copy():
+        src = slot(2, LAST).at[core_rows(1 - yh)]
+        dst = slot(3, LAST).at[0:QUART]
+        return remote(src, dst, x_send.at[1, LAST], x_recv.at[1, LAST], at.part)
+
+    def chip_sum_last():
+        if comm:
+            chip_copy(LAST).wait()
+        total = own_a[LAST] + slot(1, LAST)[...].astype(F32)
+        own_a[LAST] = total
+        slot(2, LAST)[...] = total.astype(BF)
+        if comm:
+            last_copy().start()
+
+    def input_back_last():
+        if comm:
+            last_copy().wait()
+        e = own_a[LAST, core_rows(yh), :] + slot(3, LAST)[0:QUART, :].astype(F32)
+        grad, n = norm_back(x_ref[LAST, yh, c].astype(F32), e, gain1)
+        add_small(GAIN1, col_sum(e * n))
+        add_small(SHIFT1, col_sum(e))
+        small_part()
+        gin[LAST, yh, c] = (mlow[LAST, yh, c].astype(F32) + grad).astype(BF)
+        gather_start(7, row_block(gin, LAST))
 
     def small_copy(i, slots, slot, device):
         ref = slots.at[slot]
@@ -802,8 +819,7 @@
 
     def small_first():
         small_copy(0, smp, 1 - yh, at.part).wait_recv()
-        row = small_row()
-        smx[first_slot()] = jnp.where((row >= GAIN2) & (row < BUP), smp[0] + smp[1], sm[...])
+        smx[first_slot()] = jnp.where(small_row() < BUP, smp[0] + smp[1], sm[...])
         for k in range(1, 8):
             small_copy(1, smx, first_slot(), at.core_and_x(k)).start()
 
@@ -901,7 +917,6 @@
     for s in range(SEQS):
         gather_drain(s, att_block(s))
     middle_back(2)
-    small_part()
     share_wait(3, mlow, 0)
 
     def attend_back_all(s, _):
@@ -957,51 +972,49 @@
     lax.fori_loop(0, SEQS, attend_back_all, 0)
     qkv_grads(0, HALF)
     reduce_step("start", d_att[0])
+    chip_sum_last()
     qkv_grads(HALF, HALF)
     reduce_step("start", d_att[1])
     qkv_grads(2 * HALF, 64)
     out_grads()
     reduce_step("start", d_att[2])
-    chip_sum(2, own_a.at[2])
-    reduce_step("fourth", d_down)
+    output_rows(1)
     input_back(0)
     for s in (1, 2):
         gather_drain(4 + s, row_block(mlow, s))
-    reduce_step("second", d_att[0])
-    reduce_step("second", d_att[1])
-    reduce_step("second", d_att[2])
+    reduce_step("fourth", d_down)
+    for part in d_att:
+        reduce_step("second", part)
     reduce_step("fifth", d_down)
     input_back(1)
     for part in d_att:
         reduce_step("third", part)
-    output_rows(1)
-    input_back(2)
+    input_back_last()
+    output_rows(2)
+    for part in d_att:
+        reduce_step("fourth", part)
     if comm:
         small_first()
-    reduce_step("fourth", d_att[0])
-    reduce_step("fourth", d_att[1])
-    reduce_step("fourth", d_att[2])
-    output_rows(2)
-    for s in range(SEQS):
+    for s in range(LAST):
         share_wait(s, gin, s)
     share_wait(4, res, 0)
-    reduce_step("fifth", d_att[0])
+    for part in d_att:
+        reduce_step("fifth", part)
     if comm:
         small_second()
-    reduce_step("fifth", d_att[1])
-    reduce_step("fifth", d_att[2])
     gather_forward(8, row_block(res, 1))
+    gather_forward(7, row_block(gin, LAST))
     reduce_step("finish", d_up)
     reduce_step("drain", d_up)
+    if comm:
+        for i, ref, s in ((0, gin, 0), (1, gin, 1), (3, mlow, 0), (4, res, 0)):
+            share_copy(i, ref, s, c).wait_send()
     gather_forward(9, row_block(res, 2))
     reduce_step("finish", d_down)
     reduce_step("drain", d_down)
-    if comm:
-        for i, ref, s in ((0, gin, 0), (1, gin, 1), (2, gin, 2), (3, mlow, 0), (4, res, 0)):
-            share_copy(i, ref, s, c).wait_send()
-    for s in (1, 2):
-        gather_wait(7 + s, row_block(res, s))
-        gather_drain(7 + s, row_block(res, s))
+    for i, ref, s in ((7, gin, LAST), (8, res, 1), (9, res, 2)):
+        gather_wait(i, row_block(ref, s))
+        gather_drain(i, row_block(ref, s))
     if comm:
         small_end()
         small_drain()
@@ -1111,7 +1124,7 @@
 def results(out, gin, g_up, g_down, g_qkv, small):
     def kernel(out, gin, up, down, qkv, small, *rest):
         (out_to, gin_to, qkv_to, out_w_to, up_to, down_to, bqv_to), rest = rest[:7], rest[7:]
-        vectors, (wide, sem) = rest[:7], rest[7:]
+        vectors, (wide, narrow, pair, sem) = rest[:7], rest[7:]
         copies = []
 
         def start(i, src, dst):
@@ -1132,10 +1145,12 @@
             at = (0, D, 2 * D, 2 * D + 576)[i]
             wide[at : at + rows, :] = src[first : first + rows, :].astype(F32)
             start(2 + i, wide.at[pl.ds(at, rows)], dst)
-        for row, ref in zip((GAIN1, SHIFT1, BOUT, GAIN2, SHIFT2, BUP, BDOWN), vectors):
-            ref[...] = small[row : row + 1, :].reshape(D)
-        bqv_to[0:1, :] = small[BQV : BQV + 1, 0:192]
-        bqv_to[1:2, :] = small[BQV : BQV + 1, 256:448]
+        for i, row in enumerate((GAIN1, SHIFT1, BOUT, GAIN2, SHIFT2, BUP, BDOWN)):
+            narrow[i][...] = small[row : row + 1, :].reshape(D)
+            start(6 + i, narrow[i], vectors[i])
+        pair[0:1, :] = small[BQV : BQV + 1, 0:192]
+        pair[1:2, :] = small[BQV : BQV + 1, 256:448]
+        start(13, pair, bqv_to)
         for copy in copies:
             copy.wait()
 
@@ -1158,8 +1173,13 @@
         )
         + (shape(D),) * 7,
         in_specs=[vmem] * 6,
-        out_specs=(anywhere,) * 6 + (vmem,) * 8,
-        scratch_shapes=[pltpu.VMEM((3 * D, D), F32), pltpu.SemaphoreType.DMA((6,))],
+        out_specs=(anywhere,) * 14,
+        scratch_shapes=[
+            pltpu.VMEM((3 * D, D), F32),
+            [pltpu.VMEM((D,), F32)] * 7,
+            pltpu.VMEM((2, 192), F32),
+            pltpu.SemaphoreType.DMA((14,)),
+        ],
         compiler_params=pltpu.CompilerParams(vmem_limit_bytes=12 * 2**20),
         name="results",
     )(

time: 109 us -> 105 us (0.963)
  Pallas kernels: 108 us -> 104 us
    pallas_call x1, Pallas kernels: 103 us -> 99.9 us  [layer(): pl.pallas_call(functools.partial(kernel, comm), out_shape=(pltpu.VMEM(row...]
where the time goes in v4:
time: 105 us
  Pallas kernels  104 us (99%)
    pallas_call x1, Pallas kernels, layer(): pl.pallas_call(functools.partial(kernel, comm), out_shape=(pltpu.VMEM(row...  99.9 us
    pallas_call x1, Pallas kernels, results(): pl.pallas_call(kernel, out_shape=(shape(*out.shape, dtype=BF), shape(*gin...  4.47 us

profile of v4, /device:TPU:0, one launch (start us, length us, event | category | flops | bytes accessed | tf_op | source)
XLA Modules:
  0.0 105.3 jit_solution(17711407630183450206)
XLA Ops:
  0.7 99.9 %layer.1 = (bf16[3,2,2,128,768]{4,3,2,1,0:T(8,128)(2,1)S(1)}, bf16[3,2,2,128,768]{4,3,2,1,0:T(8,128)(2,1)S(1)}, bf16[768,768]{1,0:T(8,128)(2,1)S(1)}, bf16[768,7...) custom-call(bf16[3,2,2,128,768]{4,3,2,1,0:T(8,128)(2,1)} %bitcast.8, ...), custom_call_target="tpu_custom_call" | custom-call | flops 20000000000 | bytes 20000000 | tf_op jit(solution)/shard_map/layer/pallas_call | solution.py:1099
  100.6 4.5 %results.1 = (bf16[3,2,2,128,768]{4,3,2,1,0:T(8,128)(2,1)}, bf16[3,2,2,128,768]{4,3,2,1,0:T(8,128)(2,1)}, f32[576,768]{1,0:T(8,128)}, f32[192,768]{1,0:T(8,128)}...) custom-call(bf16[3,2,2,128,768]{4,3,2,1,0:T(8,128)(2,1)S(1)} %get-tu, ...), custom_call_target="tpu_custom_call" | custom-call | tf_op jit(solution)/shard_map/results/pallas_call | solution.py:1163

commit v5 on v4

--- a/solution.py
+++ b/solution.py
@@ -74,6 +74,7 @@
         self.sib = (dp, self.t_sib)
         self.part = (dp, self.t_part)
         self.ypeer = (dp + 4 - 8 * self.yl, t)
+        self.near = (dp + 4 - 8 * self.yl, self.t_part)
         self.dp = dp
 
     def xpeer(self, j):
@@ -92,7 +93,7 @@
 
     def peers(self):
         return (
-            [self.part]
+            [self.part, self.near]
             + [self.core_and_x(k) for k in range(1, 5)]
             + [self.y_and_z(k) for k in range(1, 5)]
         )
@@ -397,7 +398,7 @@
     def fetch_y(i):
         if i == 2:
             ref = wout_rows(t, at.x * 48, 48)
-            return fetch_copy(0, ref, ref, at.part)
+            return fetch_copy(0, ref, ref, at.near)
         src, dst = ((wup, fwup), (wdown, fwdown))[i]
         some = fetch_part(i, 1)
         return fetch_copy(1, src.at[some], dst.at[some], at.part)

time: 105 us -> 105 us (level)
  no operation moved by 1% of the time
where the time goes in v5:
time: 105 us
  Pallas kernels  104 us (99%)
    pallas_call x1, Pallas kernels, layer(): pl.pallas_call(functools.partial(kernel, comm), out_shape=(pltpu.VMEM(row...  99.9 us
    pallas_call x1, Pallas kernels, results(): pl.pallas_call(kernel, out_shape=(shape(*out.shape, dtype=BF), shape(*gin...  4.47 us

profile of v5, /device:TPU:0, one launch (start us, length us, event | category | flops | bytes accessed | tf_op | source)
XLA Modules:
  0.0 105.3 jit_solution(10272850941137021576)
XLA Ops:
  0.7 99.9 %layer.1 = (bf16[3,2,2,128,768]{4,3,2,1,0:T(8,128)(2,1)S(1)}, bf16[3,2,2,128,768]{4,3,2,1,0:T(8,128)(2,1)S(1)}, bf16[768,768]{1,0:T(8,128)(2,1)S(1)}, bf16[768,7...) custom-call(bf16[3,2,2,128,768]{4,3,2,1,0:T(8,128)(2,1)} %bitcast.8, ...), custom_call_target="tpu_custom_call" | custom-call | flops 20000000000 | bytes 20000000 | tf_op jit(solution)/shard_map/layer/pallas_call | solution.py:1100
  100.6 4.5 %results.1 = (bf16[3,2,2,128,768]{4,3,2,1,0:T(8,128)(2,1)}, bf16[3,2,2,128,768]{4,3,2,1,0:T(8,128)(2,1)}, f32[576,768]{1,0:T(8,128)}, f32[192,768]{1,0:T(8,128)}...) custom-call(bf16[3,2,2,128,768]{4,3,2,1,0:T(8,128)(2,1)S(1)} %get-tu, ...), custom_call_target="tpu_custom_call" | custom-call | tf_op jit(solution)/shard_map/results/pallas_call | solution.py:1164

commit v6 on v5

--- a/solution.py
+++ b/solution.py
@@ -772,30 +772,31 @@
 
     LAST = SEQS - 1
 
-    def last_copy():
-        src = slot(2, LAST).at[core_rows(1 - yh)]
-        dst = slot(3, LAST).at[0:QUART]
-        return remote(src, dst, x_send.at[1, LAST], x_recv.at[1, LAST], at.part)
-
-    def chip_sum_last():
-        if comm:
-            chip_copy(LAST).wait()
-        total = own_a[LAST] + slot(1, LAST)[...].astype(F32)
-        own_a[LAST] = total
-        slot(2, LAST)[...] = total.astype(BF)
-        if comm:
-            last_copy().start()
-
-    def input_back_last():
-        if comm:
-            last_copy().wait()
-        e = own_a[LAST, core_rows(yh), :] + slot(3, LAST)[0:QUART, :].astype(F32)
-        grad, n = norm_back(x_ref[LAST, yh, c].astype(F32), e, gain1)
+    def later_copy(s):
+        src = slot(2, s).at[core_rows(1 - yh)]
+        dst = slot(3, s).at[0:QUART]
+        return remote(src, dst, x_send.at[1, s], x_recv.at[1, s], at.part)
+
+    def chip_sum_later(s):
+        if comm:
+            chip_copy(s).wait()
+        total = own_a[s] + slot(1, s)[...].astype(F32)
+        own_a[s] = total
+        slot(2, s)[...] = total.astype(BF)
+        if comm:
+            later_copy(s).start()
+
+    def input_back_later(s):
+        if comm:
+            later_copy(s).wait()
+        e = own_a[s, core_rows(yh), :] + slot(3, s)[0:QUART, :].astype(F32)
+        grad, n = norm_back(x_ref[s, yh, c].astype(F32), e, gain1)
         add_small(GAIN1, col_sum(e * n))
         add_small(SHIFT1, col_sum(e))
-        small_part()
-        gin[LAST, yh, c] = (mlow[LAST, yh, c].astype(F32) + grad).astype(BF)
-        gather_start(7, row_block(gin, LAST))
+        if s == LAST:
+            small_part()
+        gin[s, yh, c] = (mlow[s, yh, c].astype(F32) + grad).astype(BF)
+        gather_start(7 if s == LAST else 4, row_block(gin, s))
 
     def small_copy(i, slots, slot, device):
         ref = slots.at[slot]
@@ -932,7 +933,7 @@
                 @pl.when(s == 2)
                 def _():
                     reduce_step("fifth", d_up)
-                    chip_sum(1, own_a.at[1])
+                    chip_sum_later(1)
 
             if h == 1:
 
@@ -973,7 +974,7 @@
     lax.fori_loop(0, SEQS, attend_back_all, 0)
     qkv_grads(0, HALF)
     reduce_step("start", d_att[0])
-    chip_sum_last()
+    chip_sum_later(LAST)
     qkv_grads(HALF, HALF)
     reduce_step("start", d_att[1])
     qkv_grads(2 * HALF, 64)
@@ -981,39 +982,39 @@
     reduce_step("start", d_att[2])
     output_rows(1)
     input_back(0)
+    input_back_later(1)
     for s in (1, 2):
         gather_drain(4 + s, row_block(mlow, s))
     reduce_step("fourth", d_down)
     for part in d_att:
         reduce_step("second", part)
     reduce_step("fifth", d_down)
-    input_back(1)
     for part in d_att:
         reduce_step("third", part)
-    input_back_last()
+    input_back_later(LAST)
     output_rows(2)
     for part in d_att:
         reduce_step("fourth", part)
     if comm:
         small_first()
-    for s in range(LAST):
-        share_wait(s, gin, s)
+    share_wait(0, gin, 0)
     share_wait(4, res, 0)
     for part in d_att:
         reduce_step("fifth", part)
     if comm:
         small_second()
     gather_forward(8, row_block(res, 1))
+    gather_forward(4, row_block(gin, 1))
     gather_forward(7, row_block(gin, LAST))
     reduce_step("finish", d_up)
     reduce_step("drain", d_up)
     if comm:
-        for i, ref, s in ((0, gin, 0), (1, gin, 1), (3, mlow, 0), (4, res, 0)):
+        for i, ref, s in ((0, gin, 0), (3, mlow, 0), (4, res, 0)):
             share_copy(i, ref, s, c).wait_send()
     gather_forward(9, row_block(res, 2))
     reduce_step("finish", d_down)
     reduce_step("drain", d_down)
-    for i, ref, s in ((7, gin, LAST), (8, res, 1), (9, res, 2)):
+    for i, ref, s in ((8, res, 1), (4, gin, 1), (7, gin, LAST), (9, res, 2)):
         gather_wait(i, row_block(ref, s))
         gather_drain(i, row_block(ref, s))
     if comm:

time: 105 us -> 105 us (level)
  no operation moved by 1% of the time
where the time goes in v6:
time: 105 us
  Pallas kernels  104 us (99%)
    pallas_call x1, Pallas kernels, layer(): pl.pallas_call(functools.partial(kernel, comm), out_shape=(pltpu.VMEM(row...  99.6 us
    pallas_call x1, Pallas kernels, results(): pl.pallas_call(kernel, out_shape=(shape(*out.shape, dtype=BF), shape(*gin...  4.47 us

profile of v6, /device:TPU:0, one launch (start us, length us, event | category | flops | bytes accessed | tf_op | source)
XLA Modules:
  0.0 104.9 jit_solution(2616240689164847779)
XLA Ops:
  0.7 99.6 %layer.1 = (bf16[3,2,2,128,768]{4,3,2,1,0:T(8,128)(2,1)S(1)}, bf16[3,2,2,128,768]{4,3,2,1,0:T(8,128)(2,1)S(1)}, bf16[768,768]{1,0:T(8,128)(2,1)S(1)}, bf16[768,7...) custom-call(bf16[3,2,2,128,768]{4,3,2,1,0:T(8,128)(2,1)} %bitcast.8, ...), custom_call_target="tpu_custom_call" | custom-call | flops 20000000000 | bytes 20000000 | tf_op jit(solution)/shard_map/layer/pallas_call | solution.py:1101
  100.3 4.5 %results.1 = (bf16[3,2,2,128,768]{4,3,2,1,0:T(8,128)(2,1)}, bf16[3,2,2,128,768]{4,3,2,1,0:T(8,128)(2,1)}, f32[576,768]{1,0:T(8,128)}, f32[192,768]{1,0:T(8,128)}...) custom-call(bf16[3,2,2,128,768]{4,3,2,1,0:T(8,128)(2,1)S(1)} %get-tu, ...), custom_call_target="tpu_custom_call" | custom-call | tf_op jit(solution)/shard_map/results/pallas_call | solution.py:1165
